TPU v7x, 128 devices: a whole 4x4x4 slice. The times are simulated.
128 devices in a mesh: row: 4 (over z), col: 32 (over x, y, core).
Axes of the slice: x: 4, y: 4, z: 4, core: 2. Of those that a mesh axis runs over, the one named last changes fastest.
Arguments:
- features: bfloat16 [49152, 128], P(('row', 'col')), may hold values from -6 to 6
- weight: bfloat16 [128, 128], replicated, may hold values from -0.5 to 0.5
- tiles: bfloat16 [4, 8192, 128, 128], P('row', 'col'), may hold values from -0.09375 to 0.09375
- tile_dest: int32 [4, 8192], P('row', 'col'), may hold values from 0 to 95, as said below
- tile_src: int32 [4, 8192], P('row', 'col'), may hold values from 0 to 11, as said below
- tile_count: int32 [4, 32], P('row', 'col'), may hold values from 32 to 256, as said below
- source_of: int32 [49152], P(('row', 'col')), may hold values from 0 to 49151, as said below
- out_grad: bfloat16 [49152, 128], P(('row', 'col')), may hold values from -6 to 6
Outputs:
- activations: bfloat16 [49152, 128], P(('row', 'col'))
- feature_grad: bfloat16 [49152, 128], P(('row', 'col'))
- weight_grad: float32 [128, 128], replicated
Inputs may be any that keep to these rules, and one draw needn't show every extreme that they name: `tile_dest`: the slots of one device name distinct tiles. `tile_src`: the slots of one device name distinct tiles. `tile_count`: some device has all of its 256 slots live. `source_of`: a permutation of the 49152 vertices; of the 384 destination positions of each device, exactly 3 hold source vertices of each device.
All inputs are finite; a program needn't handle non-finite values.
Results may differ from a plain program's by a relative error of at most 0.017.
Values may be sent and summed in bfloat16 or wider, within the bound.
A program may use at most 64 MiB of HBM per device.

v0:
```python
import math

import jax
import jax.numpy as jnp
from jax import lax
from jax.sharding import PartitionSpec as P


def silu_slope(values):
    sigma = jax.nn.sigmoid(values)
    return sigma * (1.0 + values * (1.0 - sigma))


def tile_products(tile_set, dest_index, source_index, live_count, operand, out_blocks, transposed):
    tile_edge = tile_set.shape[-1]
    feat_width = operand.shape[-1]
    block_size = math.gcd(tile_set.shape[0], 32)
    operand_blocks = operand.reshape(-1, tile_edge, feat_width)
    step_count = (live_count + block_size - 1) // block_size

    def add_block(block_step, totals):
        first_slot = block_step * block_size
        tile_block = lax.dynamic_slice_in_dim(tile_set, first_slot, block_size, 0)
        dest_block = lax.dynamic_slice_in_dim(dest_index, first_slot, block_size, 0)
        source_block = lax.dynamic_slice_in_dim(source_index, first_slot, block_size, 0)
        live_mask = first_slot + jnp.arange(block_size) < live_count
        if transposed:
            product = jnp.einsum(
                "bji,bjf->bif",
                tile_block,
                operand_blocks[dest_block],
                preferred_element_type=jnp.float32,
            )
            target = source_block
        else:
            product = jnp.einsum(
                "bij,bjf->bif",
                tile_block,
                operand_blocks[source_block],
                preferred_element_type=jnp.float32,
            )
            target = dest_block
        product = jnp.where(live_mask[:, None, None], product, 0.0)
        return totals.at[target].add(product)

    totals = jnp.zeros((out_blocks, tile_edge, feat_width), jnp.float32)
    totals = lax.fori_loop(0, step_count, add_block, totals)
    return totals.reshape(-1, feat_width)


def local(features, weight, tiles, tile_dest, tile_src, tile_count, source_of, out_grad):
    shard_rows, feat_width = features.shape
    tile_edge = tiles.shape[-1]
    group_total = lax.axis_size(("row", "col"))
    strip_total = lax.axis_size("row")
    column_total = lax.axis_size("col")
    live_count = tile_count[0, 0]
    hidden = jnp.dot(features, weight, preferred_element_type=jnp.float32).astype(jnp.bfloat16)
    group_rows = lax.all_gather(hidden, "row", axis=0, tiled=True)
    partial_value = tile_products(
        tiles[0],
        tile_dest[0],
        tile_src[0],
        live_count,
        group_rows,
        column_total * shard_rows // tile_edge,
        False,
    )
    own_base = lax.axis_index(("row", "col")) * shard_rows
    summed = lax.psum_scatter(
        partial_value.astype(jnp.bfloat16), "col", scatter_dimension=0, tiled=True
    )
    row_owner = source_of // shard_rows
    send_order = jnp.argsort(row_owner, stable=True)
    got_rows, got_ids = (
        lax.all_to_all(summed[send_order], ("row", "col"), split_axis=0, concat_axis=0, tiled=True),
        lax.all_to_all(
            source_of[send_order], ("row", "col"), split_axis=0, concat_axis=0, tiled=True
        ),
    )
    local_ids = got_ids - own_base
    act_rows = jax.nn.silu(got_rows.astype(jnp.float32)).astype(jnp.bfloat16)
    activations = jnp.zeros((shard_rows, feat_width), jnp.bfloat16).at[local_ids].set(act_rows)
    returned = lax.all_to_all(
        out_grad[local_ids], ("row", "col"), split_axis=0, concat_axis=0, tiled=True
    )
    dest_grad = jnp.zeros((shard_rows, feat_width), jnp.bfloat16).at[send_order].set(returned)
    pre_float = summed.astype(jnp.float32)
    local_grad = (dest_grad.astype(jnp.float32) * silu_slope(pre_float)).astype(jnp.bfloat16)
    strip_grad = lax.all_gather(local_grad, "col", axis=0, tiled=True)
    group_partial = tile_products(
        tiles[0],
        tile_dest[0],
        tile_src[0],
        live_count,
        strip_grad,
        strip_total * shard_rows // tile_edge,
        True,
    )
    source_part = lax.psum_scatter(
        group_partial.astype(jnp.bfloat16), "row", scatter_dimension=0, tiled=True
    )
    feature_grad = jnp.dot(source_part, weight.T, preferred_element_type=jnp.float32).astype(
        jnp.bfloat16
    )
    weight_part = jnp.dot(features.T, source_part, preferred_element_type=jnp.float32)
    weight_grad = lax.psum(weight_part, ("row", "col")) * (
        1.0 / math.sqrt(shard_rows * group_total)
    )
    return (activations, feature_grad, weight_grad)


def solution(mesh):
    placed = (
        P(("row", "col"), None),
        P(),
        P("row", "col", None, None),
        P("row", "col"),
        P("row", "col"),
        P("row", "col"),
        P(("row", "col")),
        P(("row", "col"), None),
    )
    return jax.shard_map(
        local,
        mesh=mesh,
        in_specs=placed,
        out_specs=(P(("row", "col"), None), P(("row", "col"), None), P()),
        check_vma=False,
    )
```

profile of v0, /device:TPU:1, one launch (start us, length us, event | category | flops | bytes accessed | tf_op | source)
XLA Modules:
  0.0 485.0 jit_solution(11133138501414656338)
XLA Ops:
  9.0 13.5 %all_gather.6 = bf16[1536,128]{1,0:T(8,128)(2,1)} all-gather(bf16[384,128]{1,0:T(8,128)(2,1)S(1)} %convolution_convert_fusion.1), channel_id=1, replica_groups=mesh['row'=4,'col'=32] {'row'}, dimensions={0}, use_global_device_ids=true | all-gather | bytes 491520 | tf_op jit(solution)/shard_map/all_gather | solution.py:59
  22.5 3.4 broadcast_in_dim.48
  25.9 10.4 %while.20 = (s32[]{:T(128)}, f32[96,128,128]{2,1,0:T(8,128)}, s32[]{:T(128)}, s32[256]{0:T(256)S(1)}, s32[]{:T(128)}, /*index=5*/bf16[256,128,128]{2,1,0:T(8,128...) while((s32[]{:T(128)}, f32[96,128,128]{2,1,0:T(8,128)}, ...), condition=%wide.region_3.4_spmd, body=%wide.region_1.3_spmd.sunk | while | flops 135267584 | bytes 12588155 | solution.py:47
  26.0 1.7 gather_fusion
  28.4 1.7 convolution_select_fusion.4
  30.1 6.2 %scatter_fusion = f32[96,128,128]{2,1,0:T(8,128)} fusion(f32[96,128,128]{2,1,0:T(8,128)} %get-tuple-element.283, s32[32]{0:T(128)S(1)} %get-tuple-element.258, f32[32,128,128]{2,1,0:T(8,128)S(1)} %convolution_select_fusion.4), kind=kCustom, calls=%fused_computation.5.clone.1 | custom fusion | flops 524288 | bytes 6291584 | tf_op jit(solution)/shard_map/while/body/scatter-add | solution.py:44
  36.3 5.2 %convert_element_type.37 = bf16[96,128,128]{2,1,0:T(8,128)(2,1)} convert(f32[96,128,128]{2,1,0:T(8,128)} %get-tuple-element.91) | non-fusion elementwise | flops 1572864 | bytes 9437184 | tf_op jit(solution)/shard_map/convert_element_type | solution.py:71
  42.2 3.8 sort.17
  46.0 2.8 gather_fusion.2
  49.6 81.4 %all-to-all-start = ((s32[128,3,1]{1,2,0:T(1,128)}), s32[128,3,1]{1,2,0:T(1,128)S(1)}, u32[]{:S(2)}, u32[]{:S(2)}) async-start(s32[128,3,1]{1,2,0:T(1,128)} %bitcast), calls=%async_computation | async-start | bytes 131072 | tf_op jit(solution)/shard_map/all_to_all | solution.py:77
  131.1 9.5 %all-to-all-done = s32[128,3,1]{1,2,0:T(1,128)S(1)} async-done(((s32[128,3,1]{1,2,0:T(1,128)}), s32[128,3,1]{1,2,0:T(1,128)S(1)}, u32[]{:S(2)}, u32[]{:S(2)}) %all-to-all-start) | async-done | bytes 1568 | tf_op jit(solution)/shard_map/all_to_all | solution.py:77
  142.5 14.3 %all_to_all.30 = bf16[128,3,128]{2,1,0:T(4,128)(2,1)S(1)} all-to-all(bf16[128,3,128]{2,1,0:T(4,128)(2,1)S(1)} %all_to_all.24), channel_id=1, replica_groups=mesh['row'=4,'col'=32] {'row','col'}, dimensions={0} | all-to-all | bytes 196608 | tf_op jit(solution)/shard_map/all_to_all | solution.py:84
  158.5 35.0 %reduce-scatter.3.cloned.1.call-done = bf16[384,128]{1,0:T(8,128)(2,1)} async-done(((bf16[12288,128]{1,0:T(8,128)(2,1)}), bf16[384,128]{1,0:T(8,128)(2,1)}) %reduce-scatter.3.cloned.1.call-update) | async-done | bytes 98320 | tf_op jit(solution)/shard_map/reduce_scatter | solution.py:70
  195.2 11.9 %copy.18 = bf16[1,256,128,128]{2,3,1,0:T(8,128)(2,1)} copy(bf16[1,256,128,128]{3,2,1,0:T(8,128)(2,1)} %bitcast.26) | data formatting | bytes 16777216 | tf_op args[2]
  207.1 35.8 %all-gather.2.cloned.1.call-done = bf16[12288,128]{1,0:T(8,128)(2,1)} async-done(((bf16[384,128]{1,0:T(8,128)(2,1)}), bf16[12288,128]{1,0:T(8,128)(2,1)}) %all-gather.2.cloned.1.call-update) | async-done | bytes 3145744 | tf_op jit(solution)/shard_map/all_gather | solution.py:90
  243.1 9.0 %while.21 = (s32[]{:T(128)}, f32[12,128,128]{2,1,0:T(8,128)S(1)}, s32[]{:T(128)}, s32[256]{0:T(256)S(1)}, s32[]{:T(128)}, /*index=5*/bf16[256,128,128]{1,2,0:T(8...) while((s32[]{:T(128)}, f32[12,128,128]{2,1,0:T(8,128)S(1)}, ...), condition=%wide.region_9.10_spmd, body=%wide.region_7.9_spmd.sunk | while | flops 135267584 | bytes 12588155 | solution.py:47
  243.2 3.5 gather_fusion.1
  247.4 2.0 convolution_select_fusion.5
  249.3 2.7 scatter_fusion.1
  254.4 78.4 %all_to_all.31 = bf16[128,3,128]{2,1,0:T(4,128)(2,1)S(1)} all-to-all(bf16[128,3,128]{2,1,0:T(4,128)(2,1)S(1)} %all_to_all.22), channel_id=1, replica_groups=mesh['row'=4,'col'=32] {'row','col'}, dimensions={0} | all-to-all | bytes 196608 | tf_op jit(solution)/shard_map/all_to_all | solution.py:76
  333.0 2.1 scatter_custom_fusion.2
  335.1 1.7 convolution_bitcast_fusion
  336.8 1.7 convolution_convert_fusion
  338.5 138.3 %all-reduce.2.cloned.1.call-done = f32[128,128]{0,1:T(8,128)} async-done(((f32[128,128]{0,1:T(8,128)}), f32[128,128]{0,1:T(8,128)}) %all-reduce.2.cloned.1.call-update) | async-done | bytes 65552 | tf_op jit(solution)/shard_map/psum | solution.py:107
  (51 shorter events, 13.4 us)
Async XLA Ops:
  7.2 0.9 copy-start
  7.2 186.3 %reduce-scatter.3.cloned.1.call-start = ((), (), s32[]{:S(2)}) async-start(), calls=%async_computation.5 | async-start | bytes 3244032 | tf_op jit(solution)/shard_map/reduce_scatter | solution.py:70
  22.5 3.5 copy-start.5
  22.5 3.5 copy-start.6
  41.5 0.7 copy-start.1
  41.5 99.5 %copy-start.3 = (bf16[384,128]{1,0:T(8,128)(2,1)S(1)}, bf16[384,128]{1,0:T(8,128)(2,1)}, u32[]{:S(2)}) copy-start(bf16[384,128]{1,0:T(8,128)(2,1)} %param.19) | copy-start | bytes 294916
  49.6 91.0 %all-to-all-start = ((s32[128,3,1]{1,2,0:T(1,128)}), s32[128,3,1]{1,2,0:T(1,128)S(1)}, u32[]{:S(2)}, u32[]{:S(2)}) async-start(s32[128,3,1]{1,2,0:T(1,128)} %bitcast), calls=%async_computation | async-start | bytes 131072 | tf_op jit(solution)/shard_map/all_to_all | solution.py:77
  131.1 111.9 %all-gather.2.cloned.1.call-start = ((), (), s32[]{:S(2)}) async-start(), calls=%async_computation.6 | async-start | bytes 3244032 | tf_op jit(solution)/shard_map/all_gather | solution.py:90
  195.1 139.9 %reduce-scatter.5.cloned.1.call-start = ((), (), s32[]{:S(2)}) async-start(), calls=%async_computation.7 | async-start | bytes 491520 | tf_op jit(solution)/shard_map/reduce_scatter | solution.py:100
  243.0 9.9 %copy-start.2 = (bf16[384,128]{1,0:T(8,128)(2,1)S(1)}, bf16[384,128]{1,0:T(8,128)(2,1)}, u32[]{:S(2)}) copy-start(bf16[384,128]{1,0:T(8,128)(2,1)} %reduce-scatter.3.cloned.1.call-done) | copy-start | bytes 294916
  252.0 84.8 %copy-start.4 = (bf16[128,128]{1,0:T(8,128)(2,1)S(1)}, bf16[128,128]{1,0:T(8,128)(2,1)}, u32[]{:S(2)}) copy-start(bf16[128,128]{1,0:T(8,128)(2,1)} %param.13) | copy-start | bytes 98308
  252.9 224.0 %all-reduce.2.cloned.1.call-start = ((), (), s32[]{:S(2)}) async-start(), calls=%async_computation.8 | async-start | bytes 131072 | tf_op jit(solution)/shard_map/psum | solution.py:107
Sparse Core Ops, SparseCore 0:
  41.6 151.8 reduce-scatter.2
  196.6 46.3 all-gather.1
  253.0 79.6 reduce-scatter.4
  337.9 138.9 all-reduce.1
where the time goes:
time: 488 us; the launch traced here: 485 us
  waiting for transfers between devices  219 us (45%)
  blocking collectives  106 us (22%)
  starting transfers between devices  81.6 us (17%)
  local copies, waits for them, and re-layouts  30.8 us (6%)
  other arithmetic  24.9 us (5%)
  between operations  14.6 us (3%)
  matrix products  7.99 us (2%)
    psum x1, waiting for transfers between devices, local(): lax.psum(weight_part, ('row', 'col'))  138 us
    all_to_all x1, starting transfers between devices, local(): lax.all_to_all(source_of[send_order], ('row', 'col'), split_axis=0, conca...  81.4 us
    all_to_all x1, blocking collectives, local(): lax.all_to_all(summed[send_order], ('row', 'col'), split_axis=0, concat_a...  78.4 us
    all_gather x1, waiting for transfers between devices, local(): strip_grad = lax.all_gather(local_grad, 'col', axis=0, tiled=True)  35.8 us
    reduce_scatter x1, waiting for transfers between devices, local(): lax.psum_scatter(partial_value.astype(jnp.bfloat16), 'col', scatter_dimen...  35 us
    all_to_all x1, blocking collectives, local(): lax.all_to_all(out_grad[local_ids], ('row', 'col'), split_axis=0, concat_...  14.3 us
    unnamed x16, local copies, waits for them, and re-layouts  13.5 us
    all_gather x1, blocking collectives, local(): group_rows = lax.all_gather(hidden, 'row', axis=0, tiled=True)  13.5 us
  transfers between devices with their start and end apart: 5, of which 4 were waited for; matrix products, arithmetic and copies ran while one was open for 6% of the time, Pallas kernels for 0%

commit v1 on v0

v1 whole, which is shorter than its diff:
```python
import functools
import math

import jax
import jax.numpy as jnp
from jax import lax
from jax.experimental import pallas as pl
from jax.experimental.pallas import tpu as pltpu
from jax.sharding import PartitionSpec as P

MESH = pl.DeviceIdType.MESH
F32 = jnp.float32
BF16 = jnp.bfloat16
UNROLL = 8


def mm(a, b):
    return jnp.dot(a, b, preferred_element_type=F32)


def sigmoid(v):
    return 1.0 / (1.0 + jnp.exp(-v))


def iota(shape, dim):
    return lax.broadcasted_iota(jnp.int32, shape, dim)


def kernel(
    dest_s, src_s, prevd_s, prevs_s, lastd_s, lasts_s,
    feat, weight, tiles_hbm, slot_row, slot_col, id_rows, out_grad,
    act_out, fg_out, wg_out,
    tiles, run, fall, hid,
    place, place_t, regroup, regroup_t, pick, pick_t,
    id_m, id_z, id_g, id_c,
    og_m, og_c, og_g, og_z,
    ac_m, ac_z, ac_g, ac_c,
    sib_out, sib_in, x_out, y_out, x_in, y_in, x2_out, y2_out, x2_in, y2_in,
    dgrad, gath, hg_out, hg_in, hgt, dw, dw_in, dw_col, dw_colin, dw_sum, dw_all, dw_full,
    t_sem, sig,
    f_s, f_r, idz_s, idz_r, idc_s, idc_r, ogc_s, ogc_r, ogz_s, ogz_r, acz_s, acz_r, acc_s, acc_r,
    sib_s, sib_r, rx_s, rx_r, ry_s, ry_r, rx2_s, rx2_r, ry2_s, ry2_r,
    ax_s, ax_r, ay_s, ay_r, ax2_s, ax2_r, ay2_s, ay2_r, as_s, as_r,
    hg_s, hg_r, wz_s, wz_r, wc_s, wc_r, wg_s, wg_r, wa_s, wa_r,
):
    r = lax.axis_index("row")
    c = lax.axis_index("col")
    x = c // 8
    y = (c // 2) % 4
    e = c % 2
    sibling = x * 8 + y * 2 + (1 - e)

    def send(src, dst, ss, rs, row, col):
        cp = pltpu.make_async_remote_copy(
            src_ref=src, dst_ref=dst, send_sem=ss, recv_sem=rs,
            device_id={"row": row, "col": col}, device_id_type=MESH)
        cp.start()
        return cp

    def arrived(view, sem):
        pltpu.make_async_copy(view, view, sem).wait()

    def to_rows(src_of, dst, ss, rs):
        out = []
        for d in range(1, 4):
            to = lax.rem(r + d, 4)
            out.append(send(src_of(to), dst.at[r], ss.at[d - 1], rs.at[d - 1], to, c))
        return out

    def to_cols(src, dst, ss, rs):
        def one(d, carry):
            to = lax.rem(c + d, 32)
            send(src.at[to], dst.at[c], ss, rs, r, to)
            return carry
        lax.fori_loop(1, 32, one, 0)

    def cols_done(src, dst, ss, rs):
        arrived(src.at[pl.ds(0, 31)], ss)
        arrived(dst.at[pl.ds(0, 31)], rs)

    def done(copies):
        for cp in copies:
            cp.wait()

    barrier = pltpu.get_barrier_semaphore()

    def greet(d, carry):
        pl.semaphore_signal(barrier, inc=1, device_id={"row": r, "col": lax.rem(c + d, 32)}, device_id_type=MESH)
        return carry
    lax.fori_loop(1, 32, greet, 0)
    for d in range(1, 4):
        pl.semaphore_signal(barrier, inc=1, device_id={"row": lax.rem(r + d, 4), "col": c}, device_id_type=MESH)
    loads = [pltpu.make_async_copy(tiles_hbm.at[pl.ds(64 * k, 64)], tiles.at[pl.ds(64 * k, 64)], t_sem.at[k]) for k in range(4)]
    for cp in loads:
        cp.start()

    place[...] = jnp.where(iota((384, 384), 0) == slot_row[...], 1.0, 0.0).astype(BF16)
    place_t[...] = jnp.where(slot_col[...] == iota((384, 384), 1), 1.0, 0.0).astype(BF16)
    q = iota((512, 384), 0)
    s = iota((512, 384), 1)
    regroup[...] = jnp.where(((q & 3) < 3) & (s == ((q >> 2) & 3) * 96 + (q >> 4) * 3 + (q & 3)), 1.0, 0.0).astype(BF16)
    q = iota((384, 512), 1)
    s = iota((384, 512), 0)
    regroup_t[...] = jnp.where(((q & 3) < 3) & (s == ((q >> 2) & 3) * 96 + (q >> 4) * 3 + (q & 3)), 1.0, 0.0).astype(BF16)
    run[256] = jnp.zeros((128, 128), F32)
    id_m[...] = mm(place[...], id_rows[...]).astype(BF16).reshape(4, 96, 128)
    fall[r] = feat[...]
    pl.semaphore_wait(barrier, 34)

    f_copies = to_rows(lambda to: feat, fall, f_s, f_r)
    idz = to_rows(lambda to: id_m.at[to], id_z, idz_s, idz_r)
    id_z[r] = id_m[r]
    done(f_copies)
    hid[...] = mm(fall[...].reshape(1536, 128), weight[...]).astype(BF16).reshape(12, 128, 128)
    done(idz)
    id_g[...] = mm(regroup[...], id_z[...].reshape(384, 128)).astype(BF16).reshape(32, 16, 128)
    to_cols(id_g, id_c, idc_s, idc_r)
    id_c[c] = id_g[c]

    for cp in loads:
        cp.wait()

    def forward(i, carry):
        for k in range(UNROLL):
            t = i * UNROLL + k
            run[t] = run[prevd_s[t]] + mm(tiles[t], hid[src_s[t]])
        return carry
    lax.fori_loop(0, 256 // UNROLL, forward, 0)

    sib = []
    for g in range(4):
        def fill(k, carry, g=g):
            chip = g * 4 + k
            for j in range(3):
                b = (chip * 2 + (1 - e)) * 3 + j
                sib_out[chip, pl.ds(j * 128, 128), :] = run[lastd_s[b]].astype(BF16)
            return carry
        lax.fori_loop(0, 4, fill, 0)
        part = pl.ds(g * 4, 4)
        sib.append(send(sib_out.at[part], sib_in.at[part], sib_s.at[g], sib_r.at[g], r, sibling))

    cols_done(id_g, id_c, idc_s, idc_r)
    numbers = id_c[...].reshape(512, 128).astype(F32)
    col_id = (2.0 * numbers[:, 0:1] + numbers[:, 64:65]).astype(jnp.int32)
    pick[...] = jnp.where((col_id == iota((512, 384), 1)) & ((iota((512, 384), 0) & 3) < 3), 1.0, 0.0).astype(BF16)
    flipped = numbers.T
    row_id = (2.0 * flipped[0:1, :] + flipped[64:65, :]).astype(jnp.int32)
    pick_t[...] = jnp.where((row_id == iota((384, 512), 0)) & ((iota((384, 512), 1) & 3) < 3), 1.0, 0.0).astype(BF16)
    og_m[...] = mm(pick[...], out_grad[...]).astype(BF16).reshape(32, 16, 128)
    to_cols(og_m, og_c, ogc_s, ogc_r)
    og_c[c] = og_m[c]

    for g in range(4):
        sib[g].wait_recv()

        def both(k, carry, g=g):
            chip = g * 4 + k
            b = (chip * 2 + e) * 3
            rows0 = run[lastd_s[b]]
            rows1 = run[lastd_s[b + 1]]
            rows2 = run[lastd_s[b + 2]]
            got = sib_in[chip].astype(F32)
            x_out[g, k, pl.ds(0, 128), :] = (rows0 + got[0:128]).astype(BF16)
            x_out[g, k, pl.ds(128, 64), :] = (rows1[0:64] + got[128:192]).astype(BF16)
            y_out[k, g, pl.ds(0, 64), :] = (rows1[64:128] + got[192:256]).astype(BF16)
            y_out[k, g, pl.ds(64, 128), :] = (rows2 + got[256:384]).astype(BF16)
            return carry
        lax.fori_loop(0, 4, both, 0)
    for g in range(4):
        sib[g].wait_send()

    def at_chip(px, py):
        return px * 8 + py * 2 + e

    rx, ry = [], []
    for d in (2, 1, 3):
        px = lax.rem(x + d, 4)
        rx.append(send(x_out.at[px], x_in.at[x], rx_s.at[d - 1], rx_r.at[d - 1], r, at_chip(px, y)))
        py = lax.rem(y + d, 4)
        ry.append(send(y_out.at[py], y_in.at[y], ry_s.at[d - 1], ry_r.at[d - 1], r, at_chip(x, py)))

    cols_done(og_m, og_c, ogc_s, ogc_r)
    og_g[...] = mm(regroup_t[...], og_c[...].reshape(512, 128)).astype(BF16).reshape(4, 96, 128)
    ogz = to_rows(lambda to: og_g.at[to], og_z, ogz_s, ogz_r)
    og_z[r] = og_g[r]

    done(rx)

    def sum_x(k, carry):
        total = x_out[x, k].astype(F32)
        for d in range(1, 4):
            total += x_in[lax.rem(x + d, 4), k].astype(F32)
        x2_out[k] = total.astype(BF16)
        return carry
    lax.fori_loop(0, 4, sum_x, 0)
    rx2 = []
    for d in (2, 1, 3):
        py = lax.rem(y + d, 4)
        rx2.append(send(x2_out.at[py], x2_in.at[y], rx2_s.at[d - 1], rx2_r.at[d - 1], r, at_chip(x, py)))
    done(ry)

    def sum_y(k, carry):
        total = y_out[y, k].astype(F32)
        for d in range(1, 4):
            total += y_in[lax.rem(y + d, 4), k].astype(F32)
        y2_out[k] = total.astype(BF16)
        return carry
    lax.fori_loop(0, 4, sum_y, 0)
    ry2 = []
    for d in (2, 1, 3):
        px = lax.rem(x + d, 4)
        ry2.append(send(y2_out.at[px], y2_in.at[x], ry2_s.at[d - 1], ry2_r.at[d - 1], r, at_chip(px, y)))

    done(ogz)
    dgrad[...] = mm(place_t[...], og_z[...].reshape(384, 128))

    done(rx2)
    top = x2_out[y].astype(F32)
    for d in range(1, 4):
        top += x2_in[lax.rem(y + d, 4)].astype(F32)
    done(ry2)
    low = y2_out[x].astype(F32)
    for d in range(1, 4):
        low += y2_in[lax.rem(x + d, 4)].astype(F32)
    pre = jnp.concatenate([top, low], axis=0).astype(BF16).astype(F32)
    sg = sigmoid(pre)
    grad = (dgrad[...] * (sg * (1.0 + pre * (1.0 - sg)))).astype(BF16).astype(F32)
    for j in range(3):
        block = grad[j * 128:(j + 1) * 128].T.astype(BF16)
        if j == 0:
            gath[x, y, e, 0, pl.ds(0, 128), :] = block
        elif j == 1:
            gath[x, y, e, 0, pl.ds(128, 64), :] = block[0:64]
            gath[x, y, e, 1, pl.ds(0, 64), :] = block[64:128]
        else:
            gath[x, y, e, 1, pl.ds(64, 128), :] = block

    ax, ay = [], []
    for d in (2, 1, 3):
        part = gath.at[x, y, e, 0]
        ax.append(send(part, part, ax_s.at[d - 1], ax_r.at[d - 1], r, at_chip(lax.rem(x + d, 4), y)))
        part = gath.at[x, y, e, 1]
        ay.append(send(part, part, ay_s.at[d - 1], ay_r.at[d - 1], r, at_chip(x, lax.rem(y + d, 4))))
    act_rows = (pre * sg).astype(BF16)
    ac_m[...] = mm(place[...], act_rows).astype(BF16).reshape(4, 96, 128)
    acz = to_rows(lambda to: ac_m.at[to], ac_z, acz_s, acz_r)
    ac_z[r] = ac_m[r]

    done(ax)
    ax2, ay2, asib = [], [], []
    for d in (2, 1, 3):
        part = gath.at[:, y, e, 0]
        ax2.append(send(part, part, ax2_s.at[d - 1], ax2_r.at[d - 1], r, at_chip(x, lax.rem(y + d, 4))))
    done(ay)
    for d in (2, 1, 3):
        part = gath.at[x, :, e, 1]
        ay2.append(send(part, part, ay2_s.at[d - 1], ay2_r.at[d - 1], r, at_chip(lax.rem(x + d, 4), y)))
    part = gath.at[:, y, e, 0]
    asib.append(send(part, part, as_s.at[0], as_r.at[0], r, sibling))
    part = gath.at[x, :, e, 1]
    asib.append(send(part, part, as_s.at[1], as_r.at[1], r, sibling))

    done(acz)
    ac_g[...] = mm(regroup[...], ac_z[...].reshape(384, 128)).astype(BF16).reshape(32, 16, 128)
    to_cols(ac_g, ac_c, acc_s, acc_r)
    ac_c[c] = ac_g[c]

    order = (2, 1, 3)
    for n in (1, 2, 0):
        d = order[n]
        ax2[n].wait_recv()
        part = gath.at[:, lax.rem(y - d + 4, 4), e, 0]
        asib.append(send(part, part, as_s.at[1 + d], as_r.at[1 + d], r, sibling))
        ay2[n].wait_recv()
        part = gath.at[lax.rem(x - d + 4, 4), :, e, 1]
        asib.append(send(part, part, as_s.at[4 + d], as_r.at[4 + d], r, sibling))

    cols_done(ac_g, ac_c, acc_s, acc_r)
    act_out[...] = mm(pick_t[...], ac_c[...].reshape(512, 128)).astype(BF16)

    for n in range(3):
        ax2[n].wait_send()
        ay2[n].wait_send()
    done(asib)

    def backward(i, carry):
        for k in range(UNROLL):
            t = i * UNROLL + k
            b = dest_s[t]
            owner = b // 3
            j = b - owner * 3
            g = grads[b]
            run[t] = run[prevs_s[t]] + mm(g, tiles[t])
        return carry
    grads = gath.reshape(96, 128, 128)
    lax.fori_loop(0, 256 // UNROLL, backward, 0)

    def finish(k, carry):
        hg_out[k] = run[lasts_s[k]].astype(BF16)
        return carry
    lax.fori_loop(0, 12, finish, 0)
    hgc = []
    for d in (2, 1, 3):
        to = lax.rem(r + d, 4)
        hgc.append(send(hg_out.at[pl.ds(to * 3, 3)], hg_in.at[r], hg_s.at[d - 1], hg_r.at[d - 1], to, c))

    dwt = jnp.zeros((128, 128), F32)
    for k in range(12):
        dwt += mm(hg_out[k], fall[k // 3, pl.ds((k % 3) * 128, 128), :])
    dw[...] = dwt.T.reshape(4, 32, 128)
    wz = to_rows(lambda to: dw.at[to], dw_in, wz_s, wz_r)
    done(wz)
    total = dw[r]
    for d in range(1, 4):
        total += dw_in[lax.rem(r + d, 4)]
    dw_col[...] = total.reshape(32, 1, 128)
    to_cols(dw_col, dw_colin, wc_s, wc_r)
    dw_colin[c] = dw_col[c]

    done(hgc)
    for j in range(3):
        part = hg_out[r * 3 + j].astype(F32)
        for d in range(1, 4):
            part += hg_in[lax.rem(r + d, 4), j].astype(F32)
        fg_out[pl.ds(j * 128, 128), :] = mm(weight[...], part.astype(BF16)).T.astype(BF16)

    cols_done(dw_col, dw_colin, wc_s, wc_r)
    mine = jnp.sum(dw_colin[...].reshape(32, 128), axis=0, keepdims=True) * (1.0 / math.sqrt(49152.0))
    dw_sum[...] = jnp.broadcast_to(mine.reshape(1, 1, 128), (32, 1, 128))
    to_cols(dw_sum, dw_all, wg_s, wg_r)
    dw_all[c] = dw_sum[c]
    cols_done(dw_sum, dw_all, wg_s, wg_r)
    dw_full[r] = dw_all[...].reshape(32, 128)
    wa = []
    for d in (2, 1, 3):
        to = lax.rem(r + d, 4)
        wa.append(send(dw_full.at[r], dw_full.at[r], wa_s.at[d - 1], wa_r.at[d - 1], to, c))
    done(wa)
    wg_out[...] = dw_full[...].reshape(128, 128)


def local(features, weight, tiles, tile_dest, tile_src, tile_count, source_of, out_grad):
    dest, src, live = tile_dest[0], tile_src[0], tile_count[0, 0]
    at = jnp.arange(256, dtype=jnp.int32)

    def previous(key):
        same = (key[:, None] == key[None, :]) & (at[None, :] < at[:, None])
        return jnp.max(jnp.where(same, at[None, :] + 1, 0), axis=1)

    def last(key, count):
        same = (key[None, :] == jnp.arange(count, dtype=jnp.int32)[:, None]) & (at[None, :] < live)
        return jnp.max(jnp.where(same, at[None, :] + 1, 0), axis=1)

    def slot(v):
        return jnp.where(v == 0, 256, v - 1)

    owner = source_of // 384
    place = jnp.arange(384, dtype=jnp.int32)
    rank = jnp.sum(((owner[:, None] == owner[None, :]) & (place[None, :] < place[:, None])).astype(jnp.int32), axis=1)
    spot = owner * 3 + rank
    number = source_of - owner * 384
    id_rows = jnp.where(jnp.arange(128)[None, :] < 64, (number >> 1)[:, None], (number & 1)[:, None]).astype(BF16)

    def V(*shape, dtype=BF16):
        return pltpu.VMEM(shape, dtype)

    def D(n=None):
        return pltpu.SemaphoreType.DMA((n,)) if n else pltpu.SemaphoreType.DMA

    scratch = [
        V(256, 128, 128), V(257, 128, 128, dtype=F32), V(4, 384, 128), V(12, 128, 128),
        V(384, 384), V(384, 384), V(512, 384), V(384, 512), V(512, 384), V(384, 512),
        V(4, 96, 128), V(4, 96, 128), V(32, 16, 128), V(32, 16, 128),
        V(32, 16, 128), V(32, 16, 128), V(4, 96, 128), V(4, 96, 128),
        V(4, 96, 128), V(4, 96, 128), V(32, 16, 128), V(32, 16, 128),
        V(16, 384, 128), V(16, 384, 128), V(4, 4, 192, 128), V(4, 4, 192, 128), V(4, 4, 192, 128), V(4, 4, 192, 128),
        V(4, 192, 128), V(4, 192, 128), V(4, 192, 128), V(4, 192, 128),
        V(384, 128, dtype=F32), V(4, 4, 2, 2, 192, 128), V(12, 128, 128), V(4, 3, 128, 128), V(3, 128, 128),
        V(4, 32, 128, dtype=F32), V(4, 32, 128, dtype=F32), V(32, 1, 128, dtype=F32), V(32, 1, 128, dtype=F32),
        V(32, 1, 128, dtype=F32), V(32, 1, 128, dtype=F32), V(4, 32, 128, dtype=F32),
        D(4), D(),
        D(3), D(3), D(3), D(3), D(), D(), D(), D(), D(3), D(3), D(3), D(3), D(), D(),
        D(4), D(4), D(3), D(3), D(3), D(3), D(3), D(3), D(3), D(3),
        D(3), D(3), D(3), D(3), D(3), D(3), D(3), D(3), D(8), D(8),
        D(3), D(3), D(3), D(3), D(), D(), D(), D(), D(3), D(3),
    ]
    smem = pl.BlockSpec(memory_space=pltpu.SMEM)
    vmem = pl.BlockSpec(memory_space=pltpu.VMEM)
    return pl.pallas_call(
        kernel,
        out_shape=(
            jax.ShapeDtypeStruct((384, 128), BF16),
            jax.ShapeDtypeStruct((384, 128), BF16),
            jax.ShapeDtypeStruct((128, 128), F32),
        ),
        in_specs=[smem] * 6 + [vmem, vmem, pl.BlockSpec(memory_space=pl.ANY)] + [vmem] * 4,
        out_specs=(vmem, vmem, vmem),
        scratch_shapes=scratch,
        compiler_params=pltpu.CompilerParams(
            collective_id=0, has_side_effects=True, vmem_limit_bytes=56 * 2**20),
    )(
        dest, src, slot(previous(dest)), slot(previous(src)), slot(last(dest, 96)), slot(last(src, 12)),
        features, weight, tiles[0], spot[None, :], spot[:, None], id_rows, out_grad,
    )


def solution(mesh):
    placed = (
        P(("row", "col"), None),
        P(),
        P("row", "col", None, None),
        P("row", "col"),
        P("row", "col"),
        P("row", "col"),
        P(("row", "col")),
        P(("row", "col"), None),
    )
    return jax.shard_map(
        local,
        mesh=mesh,
        in_specs=placed,
        out_specs=(P(("row", "col"), None), P(("row", "col"), None), P()),
        check_vma=False,
    )
```

time: 488 us -> 107 us (0.22)
  waiting for transfers between devices: 219 us -> 0 us
  blocking collectives: 106 us -> 0 us
  Pallas kernels: 0 us -> 92.3 us
  starting transfers between devices: 81.6 us -> 0 us
  local copies, waits for them, and re-layouts: 30.8 us -> 5.9 us
  other arithmetic: 24.9 us -> 6.79 us
  between operations: 14.6 us -> 1.32 us
  matrix products: 7.99 us -> 0 us
    psum x1 -> x0, waiting for transfers between devices: 138 us -> none  [local(): lax.psum(weight_part, ('row', 'col'))]
    all_to_all x2 -> x0, blocking collectives: 92.8 us -> none  [the longest x1 78.4 us: local(): lax.all_to_all(summed[send_order], ('row', 'col'), split_axis=0, concat_a...]
    pallas_call x0 -> x1, Pallas kernels: none -> 92.3 us  [local(): pl.pallas_call(kernel, out_shape=(jax.ShapeDtypeStruct((384, 128), BF16),...]
    all_to_all x1 -> x0, starting transfers between devices: 81.4 us -> none  [local(): lax.all_to_all(source_of[send_order], ('row', 'col'), split_axis=0, conca...]
    all_gather x1 -> x0, waiting for transfers between devices: 35.8 us -> none  [local(): strip_grad = lax.all_gather(local_grad, 'col', axis=0, tiled=True)]
    reduce_scatter x2 -> x0, waiting for transfers between devices: 35 us -> none  [the longest x1 35 us: local(): lax.psum_scatter(partial_value.astype(jnp.bfloat16), 'col', scatter_dimen...]
    all_gather x1 -> x0, blocking collectives: 13.5 us -> none  [local(): group_rows = lax.all_gather(hidden, 'row', axis=0, tiled=True)]
    gather x5 -> x0, local copies, waits for them, and re-layouts: 11 us -> none  [the longest x1 3.54 us: add_block(): operand_blocks[dest_block]]
  transfers between devices with their start and end apart: 5 -> 0, of which waited for: 4 -> 0; matrix products, arithmetic and copies ran while one was open for 6% -> 0% of each run, Pallas kernels for 0% -> 0%
where the time goes in v1:
time: 107 us; the launch traced here: 106 us
  Pallas kernels  92.3 us (86%)
  other arithmetic  6.79 us (6%)
  local copies, waits for them, and re-layouts  5.9 us (6%)
  between operations  1.32 us (1%)
    pallas_call x1, Pallas kernels, local(): pl.pallas_call(kernel, out_shape=(jax.ShapeDtypeStruct((384, 128), BF16),...  92.3 us
    unnamed x3, local copies, waits for them, and re-layouts  4.55 us

profile of v1, /device:TPU:1, one launch (start us, length us, event | category | flops | bytes accessed | tf_op | source)
XLA Modules:
  0.0 106.3 jit_solution(4069893382971727974)
XLA Ops:
  1.3 0.8 select_reduce_fusion.3
  2.1 0.8 select_reduce_fusion.2
  2.9 0.6 compare_select_fusion.1.lastd_s
  3.5 0.5 compare_select_fusion.lasts_s
  4.1 1.0 select_reduce_fusion
  5.1 0.6 compare_select_fusion.2
  5.7 0.7 broadcast_shift-right-arithmetic_fusion
  6.4 0.2 convert_reduce_fusion
  6.6 0.7 broadcast_and_fusion
  7.3 0.6 broadcast_in_dim.113.slot_row
  7.9 0.8 select_convert_fusion.id_rows
  8.7 0.8 broadcast_in_dim.118.slot_col
  9.4 92.3 %shard_map.103 = (bf16[384,128]{1,0:T(8,128)(2,1)}, bf16[384,128]{1,0:T(8,128)(2,1)}, f32[128,128]{1,0:T(8,128)}) custom-call(s32[256]{0:T(256)} %bitcast.8, s32[256]{0:T(256)} %bitcast.11, s32[256]{0:T(256)} %get-tuple-element.10.prevd_s, s32[256]{0:T(256)} %get-tuple-element.9.prevs_s, s32[96]{0:T(128)} %compare_select_fusion.1.lastd_s, ...), custom_call_target="tpu_custom_call" | custom-call | tf_op jit(solution)/shard_map/pallas_call | solution.py:389
  101.8 1.5 %copy.17 = bf16[384,128]{1,0:T(8,128)(2,1)} copy(bf16[384,128]{1,0:T(8,128)(2,1)} %get-tuple-element.14) | data formatting | bytes 196608
  103.3 1.5 %copy.18 = bf16[384,128]{1,0:T(8,128)(2,1)} copy(bf16[384,128]{1,0:T(8,128)(2,1)} %get-tuple-element.15) | data formatting | bytes 196608
  104.9 1.5 %copy.19 = f32[128,128]{1,0:T(8,128)} copy(f32[128,128]{1,0:T(8,128)} %get-tuple-element.16) | data formatting | bytes 131072
  (3 shorter events, 0.0 us)

commit v2 on v1

v2 whole, which is shorter than its diff:
```python
import functools
import math

import jax
import jax.numpy as jnp
from jax import lax
from jax.experimental import pallas as pl
from jax.experimental.pallas import tpu as pltpu
from jax.sharding import PartitionSpec as P

MESH = pl.DeviceIdType.MESH
F32 = jnp.float32
BF16 = jnp.bfloat16
UNROLL = 32


def mm(a, b):
    return jnp.dot(a, b, preferred_element_type=F32)


def sigmoid(v):
    return 1.0 / (1.0 + jnp.exp(-v))


def iota(shape, dim):
    return lax.broadcasted_iota(jnp.int32, shape, dim)


def kernel(
    dest_h, src_h, count_s, owner_h, feat_h, weight_h, grad_h, tiles_h,
    act_out, fg_out, wg_out,
    tiles, run, fall, weight, out_grad, dest_v, src_v, owner_v,
    dest_s, src_s, prevd_v, prevs_v, lastd_v, lasts_v, prevd_s, prevs_s, lastd_s, lasts_s,
    place, place_t, regroup, regroup_t, pick, pick_t,
    id_m, id_z, id_g, id_c,
    og_m, og_c, og_g, og_z,
    ac_m, ac_z, ac_g, ac_c,
    sx_out, sy_out, sx_in, sy_in, x_out, y_out, x_in, y_in, x2_out, y2_out, x2_in, y2_in,
    dgrad, gath, hg_out, hg_in, dw, dw_in, dw_col, dw_colin, dw_sum, dw_all, dw_full,
    l_sem, t_sem, i_sem,
    f_s, f_r, idz_s, idz_r, idc_s, idc_r, ogc_s, ogc_r, ogz_s, ogz_r, acz_s, acz_r, acc_s, acc_r,
    sx_s, sx_r, sy_s, sy_r, rx_s, rx_r, ry_s, ry_r, rx2_s, rx2_r, ry2_s, ry2_r,
    ax_s, ax_r, ay_s, ay_r, gx_s, gx_r, gy_s, gy_r, as_s, as_r,
    hg_s, hg_r, wz_s, wz_r, wc_s, wc_r, wg_s, wg_r, wa_s, wa_r,
):
    r = lax.axis_index("row")
    c = lax.axis_index("col")
    x = c // 8
    y = (c // 2) % 4
    e = c % 2

    def at_chip(px, py):
        return {"row": r, "col": px * 8 + py * 2 + e}

    sibling = {"row": r, "col": x * 8 + y * 2 + (1 - e)}

    def send(src, dst, ss, rs, device):
        cp = pltpu.make_async_remote_copy(
            src_ref=src, dst_ref=dst, send_sem=ss, recv_sem=rs,
            device_id=device, device_id_type=MESH)
        cp.start()
        return cp

    def arrived(view, sem):
        pltpu.make_async_copy(view, view, sem).wait()

    def to_rows(src_of, dst, ss, rs):
        out = []
        for d in (2, 1, 3):
            to = lax.rem(r + d, 4)
            out.append(send(src_of(to), dst.at[r], ss.at[d - 1], rs.at[d - 1], {"row": to, "col": c}))
        return out

    def to_cols(src, dst, ss, rs):
        def one(d, carry):
            to = lax.rem(c + d, 32)
            send(src.at[to], dst.at[c], ss, rs, {"row": r, "col": to})
            return carry
        lax.fori_loop(1, 32, one, 0)

    def cols_done(src, dst, ss, rs):
        arrived(src.at[pl.ds(0, 31)], ss)
        arrived(dst.at[pl.ds(0, 31)], rs)

    def done(copies):
        for cp in copies:
            cp.wait()

    class Gather:
        def __init__(self, view, me, device, ss, rs):
            self.view, self.ss, self.rs = view, ss, rs
            self.right, self.left = lax.rem(me + 1, 4), lax.rem(me + 3, 4)
            self.to_right, self.to_left = device(self.right), device(self.left)
            self.copies = {}
            for n, half, device in ((0, 0, self.to_right), (2, 1, self.to_left), (1, 1, self.to_right), (3, 0, self.to_left)):
                self.go(n, view(me, half), device)

        def go(self, n, ref, device):
            self.copies[n] = send(ref, ref, self.ss.at[n], self.rs.at[n], device)

        def relay(self):
            self.copies[0].wait_recv()
            self.go(4, self.view(self.left, 0), self.to_right)
            self.copies[2].wait_recv()
            self.go(5, self.view(self.right, 1), self.to_left)

        def near(self):
            self.copies[1].wait_recv()
            self.copies[3].wait_recv()

        def far(self):
            self.copies[4].wait_recv()
            self.copies[5].wait_recv()

        def sent(self):
            for n in range(6):
                self.copies[n].wait_send()

    class Reduce:
        def __init__(self, out, into, half, me, device, ss, rs):
            self.out, self.into, self.half, self.me = out, into, half, me
            self.ss, self.rs = ss, rs
            self.right, self.left = lax.rem(me + 1, 4), lax.rem(me + 3, 4)
            self.across = lax.rem(me + 2, 4)
            self.to_right, self.to_left = device(self.right), device(self.left)
            self.copies = {}

        def go(self, n, pos, half, device):
            self.copies[n] = send(
                self.out.at[(pos,) + self.half(half)], self.into.at[n], self.ss.at[n], self.rs.at[n], device)

        def send_across(self):
            self.go(0, self.across, 0, self.to_right)
            self.go(2, self.across, 1, self.to_left)

        def send_right(self):
            self.go(1, self.right, 1, self.to_right)

        def send_left(self):
            self.go(3, self.left, 0, self.to_left)

        def relay(self):
            for n, pos, half, device in ((0, self.right, 0, self.to_right), (2, self.left, 1, self.to_left)):
                self.copies[n].wait_recv()
                at = (pos,) + self.half(half)
                self.out[at] = (self.out[at].astype(F32) + self.into[n].astype(F32)).astype(BF16)
                self.go(4 + n // 2, pos, half, device)

        def total(self, half):
            first, second = ((3, 4), (1, 5))[half]
            self.copies[first].wait_recv()
            own = self.out[(self.me,) + self.half(half)].astype(F32) + self.into[first].astype(F32)
            self.copies[second].wait_recv()
            return own + self.into[second].astype(F32)

        def sent(self):
            for n in range(6):
                self.copies[n].wait_send()

    barrier = pltpu.get_barrier_semaphore()

    def greet(d, carry):
        pl.semaphore_signal(barrier, inc=1, device_id={"row": r, "col": lax.rem(c + d, 32)}, device_id_type=MESH)
        return carry
    lax.fori_loop(1, 32, greet, 0)
    for d in range(1, 4):
        pl.semaphore_signal(barrier, inc=1, device_id={"row": lax.rem(r + d, 4), "col": c}, device_id_type=MESH)

    def load(n, src, dst):
        cp = pltpu.make_async_copy(src, dst, l_sem.at[n])
        cp.start()
        return cp

    feat_load = load(0, feat_h, fall.at[r])
    key_loads = [load(1, dest_h, dest_v), load(2, src_h, src_v), load(3, owner_h, owner_v)]
    scalar_loads = [load(4, dest_h, dest_s), load(5, src_h, src_s)]
    later_loads = [load(6, weight_h, weight), load(7, grad_h, out_grad)]
    tile_loads = [pltpu.make_async_copy(tiles_h.at[pl.ds(64 * k, 64)], tiles.at[pl.ds(64 * k, 64)], t_sem.at[k]) for k in range(4)]
    for cp in tile_loads:
        cp.start()
    feat_load.wait()
    pl.semaphore_wait(barrier, 34)

    half_rows = (pl.ds(0, 192), pl.ds(192, 192))
    features = Gather(lambda pos, half: fall.at[pos, half_rows[half]], r, lambda pos: {"row": pos, "col": c}, f_s, f_r)
    done(key_loads)

    source_of = owner_v[...].reshape(1, 384).astype(F32)
    owner = jnp.floor((source_of + 0.5) * (1.0 / 384.0))
    number = source_of - owner * 384.0
    owner_all = jnp.broadcast_to(owner, (384, 384))
    earlier = (owner_all.T == owner_all) & (iota((384, 384), 0) < iota((384, 384), 1))
    rank = jnp.sum(jnp.where(earlier, 1.0, 0.0), axis=0, keepdims=True)
    spot = owner * 3.0 + rank
    spots = jnp.where(iota((384, 384), 0).astype(F32) == spot, 1.0, 0.0)
    place[...] = spots.astype(BF16)
    sent_id = jnp.sum(spots * number, axis=1, keepdims=True)
    upper = jnp.floor(sent_id * 0.5)
    id_m[...] = jnp.where(iota((384, 128), 1) < 64, upper, sent_id - 2.0 * upper).astype(BF16).reshape(4, 96, 128)
    idz = to_rows(lambda to: id_m.at[to], id_z, idz_s, idz_r)
    id_z[r] = id_m[r]

    live = count_s[0, 0]

    def chains(key_v, prev_v, last_v, prev_s, last_s, n):
        key = jnp.broadcast_to(key_v[...], (256, 256))
        flipped = key.T
        at = iota((256, 256), 0)
        before = jnp.where((flipped == key) & (at < iota((256, 256), 1)), at, -1)
        best = jnp.max(before, axis=0, keepdims=True)
        prev_v[...] = jnp.where(best < 0, 256, best)
        at = iota((256, 128), 0)
        named = jnp.where((flipped[:, 0:128] == iota((256, 128), 1)) & (at < live), at, -1)
        best = jnp.max(named, axis=0, keepdims=True)
        last_v[...] = jnp.where(best < 0, 256, best)
        return [pltpu.make_async_copy(prev_v, prev_s, i_sem.at[n]), pltpu.make_async_copy(last_v, last_s, i_sem.at[n + 1])]

    index_loads = chains(dest_v, prevd_v, lastd_v, prevd_s, lastd_s, 0) + chains(src_v, prevs_v, lasts_v, prevs_s, lasts_s, 2)
    for cp in index_loads:
        cp.start()

    features.relay()
    run[256] = jnp.zeros((128, 128), F32)
    q = iota((512, 384), 0)
    s = iota((512, 384), 1)
    spread = jnp.where(((q & 3) < 3) & (s == ((q >> 2) & 3) * 96 + (q >> 4) * 3 + (q & 3)), 1.0, 0.0)
    regroup[...] = spread.astype(BF16)
    regroup_t[...] = spread.T.astype(BF16)
    place_t[...] = spots.T.astype(BF16)
    done(idz)
    id_g[...] = mm(regroup[...], id_z[...].reshape(384, 128)).astype(BF16).reshape(32, 16, 128)
    to_cols(id_g, id_c, idc_s, idc_r)
    id_c[c] = id_g[c]
    done(index_loads)
    done(scalar_loads)
    done(tile_loads)
    features.near()
    features.far()

    blocks = fall.reshape(12, 128, 128)

    def forward(i, carry):
        for k in range(UNROLL):
            t = i * UNROLL + k
            run[t] = run[prevd_s[0, t]] + mm(tiles[t], blocks[src_s[0, t]])
        return carry
    lax.fori_loop(0, 256 // UNROLL, forward, 0)

    steps = (("x", 2), ("y", 2), ("x", 1), ("x", 3), ("y", 1), ("y", 3), ("x", 0), ("y", 0))

    def first_rows(chip, core):
        b = (chip * 2 + core) * 3
        return run[lastd_s[0, b]], run[lastd_s[0, b + 1], pl.ds(0, 64), :]

    def last_rows(chip, core):
        b = (chip * 2 + core) * 3
        return run[lastd_s[0, b + 1], pl.ds(64, 64), :], run[lastd_s[0, b + 2]]

    sib = {}
    for axis, d in steps:
        if axis == "x":
            g = lax.rem(x + d, 4)
            for k in range(4):
                rows0, rows1 = first_rows(g * 4 + k, 1 - e)
                sx_out[g, k, pl.ds(0, 128), :] = rows0.astype(BF16)
                sx_out[g, k, pl.ds(128, 64), :] = rows1.astype(BF16)
            sib[axis, d] = send(sx_out.at[g], sx_in.at[g], sx_s.at[d], sx_r.at[d], sibling)
        else:
            g = lax.rem(y + d, 4)
            for k in range(4):
                rows0, rows1 = last_rows(k * 4 + g, 1 - e)
                sy_out[g, k, pl.ds(0, 64), :] = rows0.astype(BF16)
                sy_out[g, k, pl.ds(64, 128), :] = rows1.astype(BF16)
            sib[axis, d] = send(sy_out.at[g], sy_in.at[g], sy_s.at[d], sy_r.at[d], sibling)

    def pair(half):
        return (pl.ds(2 * half, 2),)

    rx = Reduce(x_out, x_in, pair, x, lambda pos: at_chip(pos, y), rx_s, rx_r)
    ry = Reduce(y_out, y_in, pair, y, lambda pos: at_chip(x, pos), ry_s, ry_r)
    for axis, d in steps:
        sib[axis, d].wait_recv()
        if axis == "x":
            g = lax.rem(x + d, 4)
            for k in range(4):
                rows0, rows1 = first_rows(g * 4 + k, e)
                x_out[g, k, pl.ds(0, 128), :] = (rows0 + sx_in[g, k, pl.ds(0, 128), :].astype(F32)).astype(BF16)
                x_out[g, k, pl.ds(128, 64), :] = (rows1 + sx_in[g, k, pl.ds(128, 64), :].astype(F32)).astype(BF16)
        else:
            g = lax.rem(y + d, 4)
            for k in range(4):
                rows0, rows1 = last_rows(k * 4 + g, e)
                y_out[g, k, pl.ds(0, 64), :] = (rows0 + sy_in[g, k, pl.ds(0, 64), :].astype(F32)).astype(BF16)
                y_out[g, k, pl.ds(64, 128), :] = (rows1 + sy_in[g, k, pl.ds(64, 128), :].astype(F32)).astype(BF16)
        ring = rx if axis == "x" else ry
        if d == 2:
            ring.send_across()
        elif d == 1:
            ring.send_right()
        elif d == 3:
            ring.send_left()

    done(later_loads)
    cols_done(id_g, id_c, idc_s, idc_r)
    numbers = id_c[...].reshape(512, 128).astype(F32)
    slot_id = 2.0 * numbers[:, 0:1] + numbers[:, 64:65]
    picked = jnp.where((slot_id == iota((512, 384), 1).astype(F32)) & ((iota((512, 384), 0) & 3) < 3), 1.0, 0.0)
    pick[...] = picked.astype(BF16)
    og_m[...] = mm(pick[...], out_grad[...]).astype(BF16).reshape(32, 16, 128)
    to_cols(og_m, og_c, ogc_s, ogc_r)
    og_c[c] = og_m[c]

    rx.relay()
    ry.relay()
    pick_t[...] = picked.T.astype(BF16)
    cols_done(og_m, og_c, ogc_s, ogc_r)
    og_g[...] = mm(regroup_t[...], og_c[...].reshape(512, 128)).astype(BF16).reshape(4, 96, 128)
    ogz = to_rows(lambda to: og_g.at[to], og_z, ogz_s, ogz_r)
    og_z[r] = og_g[r]

    rx2, ry2 = [], []
    for half in range(2):
        x2_out[pl.ds(2 * half, 2)] = rx.total(half).astype(BF16)
    for d in (2, 1, 3):
        py = lax.rem(y + d, 4)
        rx2.append(send(x2_out.at[py], x2_in.at[y], rx2_s.at[d - 1], rx2_r.at[d - 1], at_chip(x, py)))
    for half in range(2):
        y2_out[pl.ds(2 * half, 2)] = ry.total(half).astype(BF16)
    for d in (2, 1, 3):
        px = lax.rem(x + d, 4)
        ry2.append(send(y2_out.at[px], y2_in.at[x], ry2_s.at[d - 1], ry2_r.at[d - 1], at_chip(px, y)))

    done(ogz)
    dgrad[...] = mm(place_t[...], og_z[...].reshape(384, 128))
    rx.sent()
    ry.sent()
    for step in steps:
        sib[step].wait_send()
    features.sent()

    done(rx2)
    top = x2_out[y].astype(F32)
    for d in range(1, 4):
        top += x2_in[lax.rem(y + d, 4)].astype(F32)
    done(ry2)
    low = y2_out[x].astype(F32)
    for d in range(1, 4):
        low += y2_in[lax.rem(x + d, 4)].astype(F32)
    sums = jnp.concatenate([top, low], axis=0)
    sums_high = sums.astype(BF16)
    sums_low = (sums - sums_high.astype(F32)).astype(BF16)
    pre = (mm(sums_high, weight[...]) + mm(sums_low, weight[...])).astype(BF16).astype(F32)
    sg = sigmoid(pre)
    grad = (dgrad[...] * (sg * (1.0 + pre * (1.0 - sg)))).astype(BF16).astype(F32)
    turned = [grad[j * 128:(j + 1) * 128].T.astype(BF16) for j in range(3)]
    gath[x, y, e, 0, pl.ds(0, 128), :] = turned[0]
    gath[x, y, e, 0, pl.ds(128, 64), :] = turned[1][0:64]
    gath[x, y, e, 1, pl.ds(0, 64), :] = turned[1][64:128]
    gath[x, y, e, 1, pl.ds(64, 128), :] = turned[2]

    ax, ay = [], []
    for d in (2, 1, 3):
        part = gath.at[x, y, e, 0]
        ax.append(send(part, part, ax_s.at[d - 1], ax_r.at[d - 1], at_chip(lax.rem(x + d, 4), y)))
        part = gath.at[x, y, e, 1]
        ay.append(send(part, part, ay_s.at[d - 1], ay_r.at[d - 1], at_chip(x, lax.rem(y + d, 4))))

    ac_m[...] = mm(place[...], (pre * sg).astype(BF16)).astype(BF16).reshape(4, 96, 128)
    acz = to_rows(lambda to: ac_m.at[to], ac_z, acz_s, acz_r)
    ac_z[r] = ac_m[r]
    term = jnp.zeros((128, 128), F32)
    for j in range(3):
        rows = slice(j * 128, (j + 1) * 128)
        term += mm(turned[j], sums_high[rows]) + mm(turned[j], sums_low[rows])
    dw[...] = term.T.reshape(4, 32, 128)
    wz = to_rows(lambda to: dw.at[to], dw_in, wz_s, wz_r)

    done(ax)
    by_y = Gather(lambda pos, half: gath.at[pl.ds(2 * half, 2), pos, e, 0], y, lambda pos: at_chip(x, pos), gy_s, gy_r)
    done(ay)
    by_x = Gather(lambda pos, half: gath.at[pos, pl.ds(2 * half, 2), e, 1], x, lambda pos: at_chip(pos, y), gx_s, gx_r)
    asib = []

    def share(n, part):
        asib.append(send(part, part, as_s.at[n], as_r.at[n], sibling))

    share(0, gath.at[:, y, e, 0])
    share(1, gath.at[x, :, e, 1])

    done(acz)
    ac_g[...] = mm(regroup[...], ac_z[...].reshape(384, 128)).astype(BF16).reshape(32, 16, 128)
    to_cols(ac_g, ac_c, acc_s, acc_r)
    ac_c[c] = ac_g[c]

    by_y.relay()
    by_x.relay()
    by_y.near()
    share(2, gath.at[:, by_y.left, e, 0])
    share(3, gath.at[:, by_y.right, e, 0])
    by_x.near()
    share(4, gath.at[by_x.left, :, e, 1])
    share(5, gath.at[by_x.right, :, e, 1])

    done(wz)
    total = dw[r]
    for d in range(1, 4):
        total += dw_in[lax.rem(r + d, 4)]
    dw_col[...] = total.reshape(32, 1, 128)
    to_cols(dw_col, dw_colin, wc_s, wc_r)
    dw_colin[c] = dw_col[c]

    by_y.far()
    share(6, gath.at[:, lax.rem(y + 2, 4), e, 0])
    by_x.far()
    share(7, gath.at[lax.rem(x + 2, 4), :, e, 1])

    cols_done(ac_g, ac_c, acc_s, acc_r)
    act_out[...] = mm(pick_t[...], ac_c[...].reshape(512, 128)).astype(BF16)
    by_y.sent()
    by_x.sent()
    done(asib)

    grads = gath.reshape(96, 128, 128)

    def backward(i, carry):
        for k in range(UNROLL):
            t = i * UNROLL + k
            run[t] = run[prevs_s[0, t]] + mm(grads[dest_s[0, t]], tiles[t])
        return carry
    lax.fori_loop(0, 128 // UNROLL, backward, 0)

    cols_done(dw_col, dw_colin, wc_s, wc_r)
    mine = jnp.sum(dw_colin[...].reshape(32, 128), axis=0, keepdims=True) * (1.0 / math.sqrt(49152.0))
    dw_sum[...] = jnp.broadcast_to(mine.reshape(1, 1, 128), (32, 1, 128))
    to_cols(dw_sum, dw_all, wg_s, wg_r)
    dw_all[c] = dw_sum[c]
    lax.fori_loop(128 // UNROLL, 256 // UNROLL, backward, 0)

    rz = Reduce(hg_out, hg_in, lambda half: (half_rows[half],), r, lambda pos: {"row": pos, "col": c}, hg_s, hg_r)

    def finish(pos):
        for j in range(3):
            hg_out[pos, pl.ds(j * 128, 128), :] = run[lasts_s[0, pos * 3 + j]].astype(BF16)

    finish(rz.across)
    rz.send_across()
    finish(rz.right)
    rz.send_right()
    finish(rz.left)
    rz.send_left()
    finish(r)

    cols_done(dw_sum, dw_all, wg_s, wg_r)
    dw_full[r] = dw_all[...].reshape(32, 128)
    wa = to_rows(lambda to: dw_full.at[r], dw_full, wa_s, wa_r)

    rz.relay()
    hidden_grad = jnp.concatenate([rz.total(0), rz.total(1)], axis=0).astype(BF16)
    for j in range(3):
        fg_out[pl.ds(j * 128, 128), :] = mm(weight[...], hidden_grad[j * 128:(j + 1) * 128]).T.astype(BF16)
    rz.sent()
    done(wa)
    wg_out[...] = dw_full[...].reshape(128, 128)


def local(features, weight, tiles, tile_dest, tile_src, tile_count, source_of, out_grad):
    def V(*shape, dtype=BF16):
        return pltpu.VMEM(shape, dtype)

    def D(*n):
        return pltpu.SemaphoreType.DMA(n) if n else pltpu.SemaphoreType.DMA

    I32 = jnp.int32
    scratch = [
        V(256, 128, 128), V(257, 128, 128, dtype=F32), V(4, 384, 128), V(128, 128), V(384, 128),
        V(1, 256, dtype=I32), V(1, 256, dtype=I32), V(384, dtype=I32),
        pltpu.SMEM((1, 256), I32), pltpu.SMEM((1, 256), I32),
        V(1, 256, dtype=I32), V(1, 256, dtype=I32), V(1, 128, dtype=I32), V(1, 128, dtype=I32),
        pltpu.SMEM((1, 256), I32), pltpu.SMEM((1, 256), I32), pltpu.SMEM((1, 128), I32), pltpu.SMEM((1, 128), I32),
        V(384, 384), V(384, 384), V(512, 384), V(384, 512), V(512, 384), V(384, 512),
        V(4, 96, 128), V(4, 96, 128), V(32, 16, 128), V(32, 16, 128),
        V(32, 16, 128), V(32, 16, 128), V(4, 96, 128), V(4, 96, 128),
        V(4, 96, 128), V(4, 96, 128), V(32, 16, 128), V(32, 16, 128),
        V(4, 4, 192, 128), V(4, 4, 192, 128), V(4, 4, 192, 128), V(4, 4, 192, 128),
        V(4, 4, 192, 128), V(4, 4, 192, 128), V(6, 2, 192, 128), V(6, 2, 192, 128),
        V(4, 192, 128), V(4, 192, 128), V(4, 192, 128), V(4, 192, 128),
        V(384, 128, dtype=F32), V(4, 4, 2, 2, 192, 128), V(4, 384, 128), V(6, 192, 128),
        V(4, 32, 128, dtype=F32), V(4, 32, 128, dtype=F32), V(32, 1, 128, dtype=F32), V(32, 1, 128, dtype=F32),
        V(32, 1, 128, dtype=F32), V(32, 1, 128, dtype=F32), V(4, 32, 128, dtype=F32),
        D(8), D(4), D(4),
        D(6), D(6), D(3), D(3), D(), D(), D(), D(), D(3), D(3), D(3), D(3), D(), D(),
        D(4), D(4), D(4), D(4), D(6), D(6), D(6), D(6), D(3), D(3), D(3), D(3),
        D(3), D(3), D(3), D(3), D(6), D(6), D(6), D(6), D(8), D(8),
        D(6), D(6), D(3), D(3), D(), D(), D(), D(), D(3), D(3),
    ]
    smem = pl.BlockSpec(memory_space=pltpu.SMEM)
    vmem = pl.BlockSpec(memory_space=pltpu.VMEM)
    where = pl.BlockSpec(memory_space=pl.ANY)
    return pl.pallas_call(
        kernel,
        out_shape=(
            jax.ShapeDtypeStruct((384, 128), BF16),
            jax.ShapeDtypeStruct((384, 128), BF16),
            jax.ShapeDtypeStruct((128, 128), F32),
        ),
        in_specs=[where, where, smem] + [where] * 5,
        out_specs=(vmem, vmem, vmem),
        scratch_shapes=scratch,
        compiler_params=pltpu.CompilerParams(
            collective_id=0, has_side_effects=True, vmem_limit_bytes=56 * 2**20),
    )(tile_dest, tile_src, tile_count, source_of, features, weight, out_grad, tiles[0])


def solution(mesh):
    placed = (
        P(("row", "col"), None),
        P(),
        P("row", "col", None, None),
        P("row", "col"),
        P("row", "col"),
        P("row", "col"),
        P(("row", "col")),
        P(("row", "col"), None),
    )
    return jax.shard_map(
        local,
        mesh=mesh,
        in_specs=placed,
        out_specs=(P(("row", "col"), None), P(("row", "col"), None), P()),
        check_vma=False,
    )
```

time: 107 us -> 72.7 us (0.68)
  Pallas kernels: 92.3 us -> 66.6 us
  other arithmetic: 6.79 us -> 0 us
  local copies, waits for them, and re-layouts: 5.9 us -> 4.55 us
    pallas_call x1, Pallas kernels: 92.3 us -> 66.6 us  [local(): pl.pallas_call(kernel, out_shape=(jax.ShapeDtypeStruct((384, 128), BF16),...]
    reduce_max x3 -> x0, other arithmetic: 2.62 us -> none  [the longest x2 1.61 us: last(): return jnp.max(jnp.where(same, at[None, :] + 1, 0), axis=1)]
    select_n x3 -> x0, other arithmetic: 1.73 us -> none  [slot(): return jnp.where(v == 0, 256, v - 1)]
    broadcast_in_dim x2 -> x0, local copies, waits for them, and re-layouts: 1.35 us -> none  [the longest x1 0.79 us: local(): spot[:, None]]
where the time goes in v2:
time: 72.7 us; the launch traced here: 72.5 us
  Pallas kernels  66.6 us (92%)
  local copies, waits for them, and re-layouts  4.55 us (6%)
  between operations  1.29 us (2%)
    pallas_call x1, Pallas kernels, local(): pl.pallas_call(kernel, out_shape=(jax.ShapeDtypeStruct((384, 128), BF16),...  66.6 us
    unnamed x3, local copies, waits for them, and re-layouts  4.55 us

profile of v2, /device:TPU:1, one launch (start us, length us, event | category | flops | bytes accessed | tf_op | source)
XLA Modules:
  0.0 72.5 jit_solution(11132261820924929562)
XLA Ops:
  1.3 66.6 %shard_map.103 = (bf16[384,128]{1,0:T(8,128)(2,1)}, bf16[384,128]{1,0:T(8,128)(2,1)}, f32[128,128]{1,0:T(8,128)}) custom-call(s32[1,256]{1,0:T(1,128)} %dest_h.1, s32[1,256]{1,0:T(1,128)} %src_h.1, s32[1,1]{1,0:T(1,128)S(6)} %copy.14.count_s, s32[384]{0:T(512)} %owner_h.1, bf16[384,128]{1,0:T(8,128)(2,1)} %feat_h.1, bf16[128,128]{1,0:T(8,128)(2,1)} %weight_h.1, ...), custom_call_target="tpu_custom_call" | custom-call | tf_op jit(solution)/shard_map/pallas_call | solution.py:499
  67.9 1.5 %copy.15 = bf16[384,128]{1,0:T(8,128)(2,1)} copy(bf16[384,128]{1,0:T(8,128)(2,1)} %get-tuple-element.6) | data formatting | bytes 196608
  69.5 1.5 %copy.16 = bf16[384,128]{1,0:T(8,128)(2,1)} copy(bf16[384,128]{1,0:T(8,128)(2,1)} %get-tuple-element.7) | data formatting | bytes 196608
  71.0 1.5 %copy.17 = f32[128,128]{1,0:T(8,128)} copy(f32[128,128]{1,0:T(8,128)} %get-tuple-element.8) | data formatting | bytes 131072

commit v3 on v2

--- a/solution.py
+++ b/solution.py
@@ -11,7 +11,7 @@
 MESH = pl.DeviceIdType.MESH
 F32 = jnp.float32
 BF16 = jnp.bfloat16
-UNROLL = 32
+UNROLL = 64
 
 
 def mm(a, b):
@@ -181,36 +181,43 @@
     feat_load.wait()
     pl.semaphore_wait(barrier, 34)
 
-    half_rows = (pl.ds(0, 192), pl.ds(192, 192))
-    features = Gather(lambda pos, half: fall.at[pos, half_rows[half]], r, lambda pos: {"row": pos, "col": c}, f_s, f_r)
+    features = to_rows(lambda to: fall.at[r], fall, f_s, f_r)
     done(key_loads)
+
+    def wide(piece):
+        return jnp.concatenate([piece] * 3, axis=1)
 
     source_of = owner_v[...].reshape(1, 384).astype(F32)
     owner = jnp.floor((source_of + 0.5) * (1.0 / 384.0))
     number = source_of - owner * 384.0
-    owner_all = jnp.broadcast_to(owner, (384, 384))
-    earlier = (owner_all.T == owner_all) & (iota((384, 384), 0) < iota((384, 384), 1))
+    owner_col = wide(jnp.broadcast_to(owner, (128, 384)).T)
+    earlier = (owner_col == owner) & (iota((384, 384), 0) < iota((384, 384), 1))
     rank = jnp.sum(jnp.where(earlier, 1.0, 0.0), axis=0, keepdims=True)
     spot = owner * 3.0 + rank
-    spots = jnp.where(iota((384, 384), 0).astype(F32) == spot, 1.0, 0.0)
-    place[...] = spots.astype(BF16)
-    sent_id = jnp.sum(spots * number, axis=1, keepdims=True)
-    upper = jnp.floor(sent_id * 0.5)
-    id_m[...] = jnp.where(iota((384, 128), 1) < 64, upper, sent_id - 2.0 * upper).astype(BF16).reshape(4, 96, 128)
+    four = owner * 4.0 + rank
+    four_col = jnp.broadcast_to(four, (128, 384)).T
+    four_col = jnp.concatenate([four_col] * 4, axis=1)
+    lanes = jnp.where(four_col == iota((384, 512), 1).astype(F32), 1.0, 0.0).astype(BF16)
+    upper = jnp.floor(number * 0.5)
+    parts = jnp.where(iota((16, 384), 0) == 0, upper, number - 2.0 * upper).astype(BF16)
+    sent = mm(parts, lanes).astype(BF16)
+    for k in range(4):
+        id_m[k] = sent[:, k * 128:(k + 1) * 128]
     idz = to_rows(lambda to: id_m.at[to], id_z, idz_s, idz_r)
     id_z[r] = id_m[r]
 
     live = count_s[0, 0]
 
     def chains(key_v, prev_v, last_v, prev_s, last_s, n):
-        key = jnp.broadcast_to(key_v[...], (256, 256))
-        flipped = key.T
+        key = key_v[...]
+        col = jnp.broadcast_to(key, (128, 256)).T
+        flipped = jnp.concatenate([col, col], axis=1)
         at = iota((256, 256), 0)
         before = jnp.where((flipped == key) & (at < iota((256, 256), 1)), at, -1)
         best = jnp.max(before, axis=0, keepdims=True)
         prev_v[...] = jnp.where(best < 0, 256, best)
         at = iota((256, 128), 0)
-        named = jnp.where((flipped[:, 0:128] == iota((256, 128), 1)) & (at < live), at, -1)
+        named = jnp.where((col == iota((256, 128), 1)) & (at < live), at, -1)
         best = jnp.max(named, axis=0, keepdims=True)
         last_v[...] = jnp.where(best < 0, 256, best)
         return [pltpu.make_async_copy(prev_v, prev_s, i_sem.at[n]), pltpu.make_async_copy(last_v, last_s, i_sem.at[n + 1])]
@@ -219,23 +226,33 @@
     for cp in index_loads:
         cp.start()
 
-    features.relay()
-    run[256] = jnp.zeros((128, 128), F32)
-    q = iota((512, 384), 0)
-    s = iota((512, 384), 1)
-    spread = jnp.where(((q & 3) < 3) & (s == ((q >> 2) & 3) * 96 + (q >> 4) * 3 + (q & 3)), 1.0, 0.0)
-    regroup[...] = spread.astype(BF16)
-    regroup_t[...] = spread.T.astype(BF16)
-    place_t[...] = spots.T.astype(BF16)
+    row = iota((512, 128), 0)
+    finds = jnp.where(iota((512, 128), 1) == (row >> 4) * 4 + (row & 3), 1.0, 0.0).astype(BF16)
     done(idz)
-    id_g[...] = mm(regroup[...], id_z[...].reshape(384, 128)).astype(BF16).reshape(32, 16, 128)
+    found = lax.dot_general(finds, id_z[...].reshape(64, 128), (((1,), (1,)), ((), ())), preferred_element_type=F32)
+    lane = iota((512, 64), 1) - ((iota((512, 64), 0) >> 2) & 3) * 16
+    upper = jnp.sum(jnp.where(lane == 0, found, 0.0), axis=1, keepdims=True)
+    lower = jnp.sum(jnp.where(lane == 1, found, 0.0), axis=1, keepdims=True)
+    id_g[...] = jnp.where(iota((512, 128), 1) < 64, upper, lower).astype(BF16).reshape(32, 16, 128)
     to_cols(id_g, id_c, idc_s, idc_r)
     id_c[c] = id_g[c]
+
+    run[256] = jnp.zeros((128, 128), F32)
+
+    def spread(q, s):
+        wanted = ((q >> 2) & 3) * 96 + (q >> 4) * 3 + (q & 3)
+        return jnp.where(((q & 3) < 3) & (s == wanted), 1.0, 0.0).astype(BF16)
+
+    regroup[...] = spread(iota((512, 384), 0), iota((512, 384), 1))
+    regroup_t[...] = spread(iota((384, 512), 1), iota((384, 512), 0))
+    place[...] = jnp.where(iota((384, 384), 0).astype(F32) == spot, 1.0, 0.0).astype(BF16)
+    spot_col = wide(jnp.broadcast_to(spot, (128, 384)).T)
+    place_t[...] = jnp.where(spot_col == iota((384, 384), 1).astype(F32), 1.0, 0.0).astype(BF16)
     done(index_loads)
     done(scalar_loads)
     done(tile_loads)
-    features.near()
-    features.far()
+    for cp in features:
+        cp.wait_recv()
 
     blocks = fall.reshape(12, 128, 128)
 
@@ -272,6 +289,18 @@
                 sy_out[g, k, pl.ds(0, 64), :] = rows0.astype(BF16)
                 sy_out[g, k, pl.ds(64, 128), :] = rows1.astype(BF16)
             sib[axis, d] = send(sy_out.at[g], sy_in.at[g], sy_s.at[d], sy_r.at[d], sibling)
+
+    done(later_loads)
+    cols_done(id_g, id_c, idc_s, idc_r)
+    numbers = id_c[...].reshape(512, 128).astype(F32)
+    swapped = jnp.concatenate([numbers[:, 64:128], numbers[:, 0:64]], axis=1)
+    low_lane = iota((512, 128), 1) < 64
+    slot_id = 2.0 * jnp.where(low_lane, numbers, swapped) + jnp.where(low_lane, swapped, numbers)
+    slot_id = jnp.where((iota((512, 128), 0) & 3) < 3, slot_id, -1.0)
+    pick[...] = jnp.where(wide(slot_id) == iota((512, 384), 1).astype(F32), 1.0, 0.0).astype(BF16)
+    og_m[...] = mm(pick[...], out_grad[...]).astype(BF16).reshape(32, 16, 128)
+    to_cols(og_m, og_c, ogc_s, ogc_r)
+    og_c[c] = og_m[c]
 
     def pair(half):
         return (pl.ds(2 * half, 2),)
@@ -300,23 +329,17 @@
         elif d == 3:
             ring.send_left()
 
-    done(later_loads)
-    cols_done(id_g, id_c, idc_s, idc_r)
-    numbers = id_c[...].reshape(512, 128).astype(F32)
-    slot_id = 2.0 * numbers[:, 0:1] + numbers[:, 64:65]
-    picked = jnp.where((slot_id == iota((512, 384), 1).astype(F32)) & ((iota((512, 384), 0) & 3) < 3), 1.0, 0.0)
-    pick[...] = picked.astype(BF16)
-    og_m[...] = mm(pick[...], out_grad[...]).astype(BF16).reshape(32, 16, 128)
-    to_cols(og_m, og_c, ogc_s, ogc_r)
-    og_c[c] = og_m[c]
-
-    rx.relay()
-    ry.relay()
-    pick_t[...] = picked.T.astype(BF16)
     cols_done(og_m, og_c, ogc_s, ogc_r)
     og_g[...] = mm(regroup_t[...], og_c[...].reshape(512, 128)).astype(BF16).reshape(4, 96, 128)
     ogz = to_rows(lambda to: og_g.at[to], og_z, ogz_s, ogz_r)
     og_z[r] = og_g[r]
+
+    rx.relay()
+    ry.relay()
+
+    slot_row = slot_id.T
+    slot_row = jnp.concatenate([slot_row] * 3, axis=0)
+    pick_t[...] = jnp.where(slot_row == iota((384, 512), 0).astype(F32), 1.0, 0.0).astype(BF16)
 
     rx2, ry2 = [], []
     for half in range(2):
@@ -336,7 +359,8 @@
     ry.sent()
     for step in steps:
         sib[step].wait_send()
-    features.sent()
+    for cp in features:
+        cp.wait_send()
 
     done(rx2)
     top = x2_out[y].astype(F32)
@@ -409,10 +433,11 @@
     to_cols(dw_col, dw_colin, wc_s, wc_r)
     dw_colin[c] = dw_col[c]
 
-    by_y.far()
-    share(6, gath.at[:, lax.rem(y + 2, 4), e, 0])
-    by_x.far()
-    share(7, gath.at[lax.rem(x + 2, 4), :, e, 1])
+    for half in range(2):
+        by_y.copies[4 + half].wait_recv()
+        share(6 + half, by_y.view(lax.rem(y + 2, 4), half))
+        by_x.copies[4 + half].wait_recv()
+        share(8 + half, by_x.view(lax.rem(x + 2, 4), half))
 
     cols_done(ac_g, ac_c, acc_s, acc_r)
     act_out[...] = mm(pick_t[...], ac_c[...].reshape(512, 128)).astype(BF16)
@@ -436,29 +461,30 @@
     dw_all[c] = dw_sum[c]
     lax.fori_loop(128 // UNROLL, 256 // UNROLL, backward, 0)
 
-    rz = Reduce(hg_out, hg_in, lambda half: (half_rows[half],), r, lambda pos: {"row": pos, "col": c}, hg_s, hg_r)
-
     def finish(pos):
         for j in range(3):
             hg_out[pos, pl.ds(j * 128, 128), :] = run[lasts_s[0, pos * 3 + j]].astype(BF16)
 
-    finish(rz.across)
-    rz.send_across()
-    finish(rz.right)
-    rz.send_right()
-    finish(rz.left)
-    rz.send_left()
+    hgc = []
+    for d in (2, 1, 3):
+        to = lax.rem(r + d, 4)
+        finish(to)
+        hgc.append(send(hg_out.at[to], hg_in.at[d - 1], hg_s.at[d - 1], hg_r.at[d - 1], {"row": to, "col": c}))
     finish(r)
 
     cols_done(dw_sum, dw_all, wg_s, wg_r)
     dw_full[r] = dw_all[...].reshape(32, 128)
     wa = to_rows(lambda to: dw_full.at[r], dw_full, wa_s, wa_r)
 
-    rz.relay()
-    hidden_grad = jnp.concatenate([rz.total(0), rz.total(1)], axis=0).astype(BF16)
+    total = hg_out[r].astype(F32)
+    for n, d in ((1, 1), (2, 3), (0, 2)):
+        hgc[n].wait_recv()
+        total += hg_in[d - 1].astype(F32)
+    hidden_grad = total.astype(BF16)
     for j in range(3):
         fg_out[pl.ds(j * 128, 128), :] = mm(weight[...], hidden_grad[j * 128:(j + 1) * 128]).T.astype(BF16)
-    rz.sent()
+    for cp in hgc:
+        cp.wait_send()
     done(wa)
     wg_out[...] = dw_full[...].reshape(128, 128)
 
@@ -478,19 +504,19 @@
         V(1, 256, dtype=I32), V(1, 256, dtype=I32), V(1, 128, dtype=I32), V(1, 128, dtype=I32),
         pltpu.SMEM((1, 256), I32), pltpu.SMEM((1, 256), I32), pltpu.SMEM((1, 128), I32), pltpu.SMEM((1, 128), I32),
         V(384, 384), V(384, 384), V(512, 384), V(384, 512), V(512, 384), V(384, 512),
-        V(4, 96, 128), V(4, 96, 128), V(32, 16, 128), V(32, 16, 128),
+        V(4, 16, 128), V(4, 16, 128), V(32, 16, 128), V(32, 16, 128),
         V(32, 16, 128), V(32, 16, 128), V(4, 96, 128), V(4, 96, 128),
         V(4, 96, 128), V(4, 96, 128), V(32, 16, 128), V(32, 16, 128),
         V(4, 4, 192, 128), V(4, 4, 192, 128), V(4, 4, 192, 128), V(4, 4, 192, 128),
         V(4, 4, 192, 128), V(4, 4, 192, 128), V(6, 2, 192, 128), V(6, 2, 192, 128),
         V(4, 192, 128), V(4, 192, 128), V(4, 192, 128), V(4, 192, 128),
-        V(384, 128, dtype=F32), V(4, 4, 2, 2, 192, 128), V(4, 384, 128), V(6, 192, 128),
+        V(384, 128, dtype=F32), V(4, 4, 2, 2, 192, 128), V(4, 384, 128), V(3, 384, 128),
         V(4, 32, 128, dtype=F32), V(4, 32, 128, dtype=F32), V(32, 1, 128, dtype=F32), V(32, 1, 128, dtype=F32),
         V(32, 1, 128, dtype=F32), V(32, 1, 128, dtype=F32), V(4, 32, 128, dtype=F32),
         D(8), D(4), D(4),
         D(6), D(6), D(3), D(3), D(), D(), D(), D(), D(3), D(3), D(3), D(3), D(), D(),
         D(4), D(4), D(4), D(4), D(6), D(6), D(6), D(6), D(3), D(3), D(3), D(3),
-        D(3), D(3), D(3), D(3), D(6), D(6), D(6), D(6), D(8), D(8),
+        D(3), D(3), D(3), D(3), D(6), D(6), D(6), D(6), D(10), D(10),
         D(6), D(6), D(3), D(3), D(), D(), D(), D(), D(3), D(3),
     ]
     smem = pl.BlockSpec(memory_space=pltpu.SMEM)
@@ -499,9 +525,9 @@
     return pl.pallas_call(
         kernel,
         out_shape=(
-            jax.ShapeDtypeStruct((384, 128), BF16),
-            jax.ShapeDtypeStruct((384, 128), BF16),
-            jax.ShapeDtypeStruct((128, 128), F32),
+            pltpu.VMEM((384, 128), BF16),
+            pltpu.VMEM((384, 128), BF16),
+            pltpu.VMEM((128, 128), F32),
         ),
         in_specs=[where, where, smem] + [where] * 5,
         out_specs=(vmem, vmem, vmem),

time: 72.7 us -> 68.5 us (0.942)
  local copies, waits for them, and re-layouts: 4.55 us -> 1.91 us
  Pallas kernels: 66.6 us -> 65.2 us
    unnamed x3, local copies, waits for them, and re-layouts: 4.55 us -> 1.91 us
    pallas_call x1, Pallas kernels: 66.6 us -> 65.2 us  [local(): pl.pallas_call(kernel, out_shape=(pltpu.VMEM((384, 128), BF16), pltpu.VME...]
where the time goes in v3:
time: 68.5 us; the launch traced here: 68.4 us
  Pallas kernels  65.2 us (95%)
  local copies, waits for them, and re-layouts  1.91 us (3%)
  between operations  1.29 us (2%)
    pallas_call x1, Pallas kernels, local(): pl.pallas_call(kernel, out_shape=(pltpu.VMEM((384, 128), BF16), pltpu.VME...  65.2 us
    unnamed x3, local copies, waits for them, and re-layouts  1.91 us

profile of v3, /device:TPU:1, one launch (start us, length us, event | category | flops | bytes accessed | tf_op | source)
XLA Modules:
  0.0 68.4 jit_solution(17730350670228299194)
XLA Ops:
  1.3 65.2 %shard_map.103 = (bf16[384,128]{1,0:T(8,128)(2,1)S(1)}, bf16[384,128]{1,0:T(8,128)(2,1)S(1)}, f32[128,128]{1,0:T(8,128)S(1)}) custom-call(s32[1,256]{1,0:T(1,128)} %dest_h.1, s32[1,256]{1,0:T(1,128)} %src_h.1, s32[1,1]{1,0:T(1,128)S(6)} %copy.17.count_s, s32[384]{0:T(512)} %owner_h.1, bf16[384,128]{1,0:T(8,128)(2,1)} %feat_h.1, bf16[128,128]{1,0:T(8,128)(2,1)} %weight_h.1, ...), custom_call_target="tpu_custom_call" | custom-call | tf_op jit(solution)/shard_map/pallas_call | solution.py:525
  66.4 0.6 copy.14
  67.1 0.6 copy.16
  67.7 0.6 copy.15

commit v4 on v3

--- a/solution.py
+++ b/solution.py
@@ -36,12 +36,12 @@
     og_m, og_c, og_g, og_z,
     ac_m, ac_z, ac_g, ac_c,
     sx_out, sy_out, sx_in, sy_in, x_out, y_out, x_in, y_in, x2_out, y2_out, x2_in, y2_in,
-    dgrad, gath, hg_out, hg_in, dw, dw_in, dw_col, dw_colin, dw_sum, dw_all, dw_full,
+    dgrad, gath, hg_out, hg_in, dw, dw_in, dw_all, dw_full, spare,
     l_sem, t_sem, i_sem,
     f_s, f_r, idz_s, idz_r, idc_s, idc_r, ogc_s, ogc_r, ogz_s, ogz_r, acz_s, acz_r, acc_s, acc_r,
     sx_s, sx_r, sy_s, sy_r, rx_s, rx_r, ry_s, ry_r, rx2_s, rx2_r, ry2_s, ry2_r,
     ax_s, ax_r, ay_s, ay_r, gx_s, gx_r, gy_s, gy_r, as_s, as_r,
-    hg_s, hg_r, wz_s, wz_r, wc_s, wc_r, wg_s, wg_r, wa_s, wa_r,
+    hg_s, hg_r, wz_s, wz_r, wg_s, wg_r, wa_s, wa_r,
 ):
     r = lax.axis_index("row")
     c = lax.axis_index("col")
@@ -179,9 +179,6 @@
     for cp in tile_loads:
         cp.start()
     feat_load.wait()
-    pl.semaphore_wait(barrier, 34)
-
-    features = to_rows(lambda to: fall.at[r], fall, f_s, f_r)
     done(key_loads)
 
     def wide(piece):
@@ -203,8 +200,12 @@
     sent = mm(parts, lanes).astype(BF16)
     for k in range(4):
         id_m[k] = sent[:, k * 128:(k + 1) * 128]
+    pl.semaphore_wait(barrier, 34)
     idz = to_rows(lambda to: id_m.at[to], id_z, idz_s, idz_r)
     id_z[r] = id_m[r]
+
+    features = to_rows(lambda to: fall.at[r], fall, f_s, f_r)
+
 
     live = count_s[0, 0]
 
@@ -244,6 +245,9 @@
         return jnp.where(((q & 3) < 3) & (s == wanted), 1.0, 0.0).astype(BF16)
 
     regroup[...] = spread(iota((512, 384), 0), iota((512, 384), 1))
+    row = iota((512, 96), 0)
+    at_spare = ((row & 3) == 3) & (iota((512, 96), 1) == ((row >> 2) & 3) * 32 + (row >> 4))
+    spare[...] = jnp.where(at_spare, 1.0, 0.0).astype(BF16)
     regroup_t[...] = spread(iota((384, 512), 1), iota((384, 512), 0))
     place[...] = jnp.where(iota((384, 384), 0).astype(F32) == spot, 1.0, 0.0).astype(BF16)
     spot_col = wide(jnp.broadcast_to(spot, (128, 384)).T)
@@ -355,10 +359,6 @@
 
     done(ogz)
     dgrad[...] = mm(place_t[...], og_z[...].reshape(384, 128))
-    rx.sent()
-    ry.sent()
-    for step in steps:
-        sib[step].wait_send()
     for cp in features:
         cp.wait_send()
 
@@ -412,7 +412,16 @@
     share(1, gath.at[x, :, e, 1])
 
     done(acz)
-    ac_g[...] = mm(regroup[...], ac_z[...].reshape(384, 128)).astype(BF16).reshape(32, 16, 128)
+    done(wz)
+    total = dw[r]
+    for d in range(1, 4):
+        total += dw_in[lax.rem(r + d, 4)]
+    high = total.astype(BF16)
+    rest = total - high.astype(F32)
+    middle = rest.astype(BF16)
+    low = (rest - middle.astype(F32)).astype(BF16)
+    ac_g[...] = (mm(regroup[...], ac_z[...].reshape(384, 128)) + mm(spare[...], jnp.concatenate([high, middle, low], axis=0))
+                 ).astype(BF16).reshape(32, 16, 128)
     to_cols(ac_g, ac_c, acc_s, acc_r)
     ac_c[c] = ac_g[c]
 
@@ -425,14 +434,6 @@
     share(4, gath.at[by_x.left, :, e, 1])
     share(5, gath.at[by_x.right, :, e, 1])
 
-    done(wz)
-    total = dw[r]
-    for d in range(1, 4):
-        total += dw_in[lax.rem(r + d, 4)]
-    dw_col[...] = total.reshape(32, 1, 128)
-    to_cols(dw_col, dw_colin, wc_s, wc_r)
-    dw_colin[c] = dw_col[c]
-
     for half in range(2):
         by_y.copies[4 + half].wait_recv()
         share(6 + half, by_y.view(lax.rem(y + 2, 4), half))
@@ -440,10 +441,14 @@
         share(8 + half, by_x.view(lax.rem(x + 2, 4), half))
 
     cols_done(ac_g, ac_c, acc_s, acc_r)
-    act_out[...] = mm(pick_t[...], ac_c[...].reshape(512, 128)).astype(BF16)
-    by_y.sent()
-    by_x.sent()
-    done(asib)
+    came = ac_c[...].reshape(512, 128)
+    act_out[...] = mm(pick_t[...], came).astype(BF16)
+    ones = jnp.where((iota((16, 512), 1) & 3) == 3, 1.0, 0.0).astype(BF16)
+    mine = mm(ones, came)[0:1] * (1.0 / math.sqrt(49152.0))
+    dw_all[x, y, e] = mine
+    w_copies = [send(dw_all.at[x, y, e], dw_all.at[x, y, e], wg_s.at[0], wg_r.at[0], sibling)]
+    for cp in asib:
+        cp.wait_recv()
 
     grads = gath.reshape(96, 128, 128)
 
@@ -454,16 +459,21 @@
         return carry
     lax.fori_loop(0, 128 // UNROLL, backward, 0)
 
-    cols_done(dw_col, dw_colin, wc_s, wc_r)
-    mine = jnp.sum(dw_colin[...].reshape(32, 128), axis=0, keepdims=True) * (1.0 / math.sqrt(49152.0))
-    dw_sum[...] = jnp.broadcast_to(mine.reshape(1, 1, 128), (32, 1, 128))
-    to_cols(dw_sum, dw_all, wg_s, wg_r)
-    dw_all[c] = dw_sum[c]
+    w_copies[0].wait_recv()
+    for d in (2, 1, 3):
+        part = dw_all.at[x, y]
+        w_copies.append(send(part, part, wg_s.at[d], wg_r.at[d], at_chip(lax.rem(x + d, 4), y)))
     lax.fori_loop(128 // UNROLL, 256 // UNROLL, backward, 0)
 
     def finish(pos):
         for j in range(3):
             hg_out[pos, pl.ds(j * 128, 128), :] = run[lasts_s[0, pos * 3 + j]].astype(BF16)
+
+    for cp in w_copies[1:]:
+        cp.wait_recv()
+    for d in (2, 1, 3):
+        part = dw_all.at[:, y]
+        w_copies.append(send(part, part, wg_s.at[3 + d], wg_r.at[3 + d], at_chip(x, lax.rem(y + d, 4))))
 
     hgc = []
     for d in (2, 1, 3):
@@ -472,10 +482,17 @@
         hgc.append(send(hg_out.at[to], hg_in.at[d - 1], hg_s.at[d - 1], hg_r.at[d - 1], {"row": to, "col": c}))
     finish(r)
 
-    cols_done(dw_sum, dw_all, wg_s, wg_r)
+    for cp in w_copies[4:]:
+        cp.wait_recv()
     dw_full[r] = dw_all[...].reshape(32, 128)
     wa = to_rows(lambda to: dw_full.at[r], dw_full, wa_s, wa_r)
 
+    by_y.sent()
+    by_x.sent()
+    rx.sent()
+    ry.sent()
+    for cp in asib + list(sib.values()):
+        cp.wait_send()
     total = hg_out[r].astype(F32)
     for n, d in ((1, 1), (2, 3), (0, 2)):
         hgc[n].wait_recv()
@@ -483,7 +500,7 @@
     hidden_grad = total.astype(BF16)
     for j in range(3):
         fg_out[pl.ds(j * 128, 128), :] = mm(weight[...], hidden_grad[j * 128:(j + 1) * 128]).T.astype(BF16)
-    for cp in hgc:
+    for cp in hgc + w_copies:
         cp.wait_send()
     done(wa)
     wg_out[...] = dw_full[...].reshape(128, 128)
@@ -511,13 +528,12 @@
         V(4, 4, 192, 128), V(4, 4, 192, 128), V(6, 2, 192, 128), V(6, 2, 192, 128),
         V(4, 192, 128), V(4, 192, 128), V(4, 192, 128), V(4, 192, 128),
         V(384, 128, dtype=F32), V(4, 4, 2, 2, 192, 128), V(4, 384, 128), V(3, 384, 128),
-        V(4, 32, 128, dtype=F32), V(4, 32, 128, dtype=F32), V(32, 1, 128, dtype=F32), V(32, 1, 128, dtype=F32),
-        V(32, 1, 128, dtype=F32), V(32, 1, 128, dtype=F32), V(4, 32, 128, dtype=F32),
+        V(4, 32, 128, dtype=F32), V(4, 32, 128, dtype=F32), V(4, 4, 2, 1, 128, dtype=F32), V(4, 32, 128, dtype=F32), V(512, 96),
         D(8), D(4), D(4),
         D(6), D(6), D(3), D(3), D(), D(), D(), D(), D(3), D(3), D(3), D(3), D(), D(),
         D(4), D(4), D(4), D(4), D(6), D(6), D(6), D(6), D(3), D(3), D(3), D(3),
         D(3), D(3), D(3), D(3), D(6), D(6), D(6), D(6), D(10), D(10),
-        D(6), D(6), D(3), D(3), D(), D(), D(), D(), D(3), D(3),
+        D(6), D(6), D(3), D(3), D(7), D(7), D(3), D(3),
     ]
     smem = pl.BlockSpec(memory_space=pltpu.SMEM)
     vmem = pl.BlockSpec(memory_space=pltpu.VMEM)

time: 68.5 us -> 66.3 us (0.968)
  Pallas kernels: 65.2 us -> 63 us
    pallas_call x1, Pallas kernels: 65.2 us -> 63 us  [local(): pl.pallas_call(kernel, out_shape=(pltpu.VMEM((384, 128), BF16), pltpu.VME...]
where the time goes in v4:
time: 66.3 us; the launch traced here: 66.2 us
  Pallas kernels  63 us (95%)
  local copies, waits for them, and re-layouts  1.91 us (3%)
  between operations  1.29 us (2%)
    pallas_call x1, Pallas kernels, local(): pl.pallas_call(kernel, out_shape=(pltpu.VMEM((384, 128), BF16), pltpu.VME...  63 us
    unnamed x3, local copies, waits for them, and re-layouts  1.91 us

profile of v4, /device:TPU:1, one launch (start us, length us, event | category | flops | bytes accessed | tf_op | source)
XLA Modules:
  0.0 66.2 jit_solution(13175618184747112617)
XLA Ops:
  1.3 63.0 %shard_map.103 = (bf16[384,128]{1,0:T(8,128)(2,1)S(1)}, bf16[384,128]{1,0:T(8,128)(2,1)S(1)}, f32[128,128]{1,0:T(8,128)S(1)}) custom-call(s32[1,256]{1,0:T(1,128)} %dest_h.1, s32[1,256]{1,0:T(1,128)} %src_h.1, s32[1,1]{1,0:T(1,128)S(6)} %copy.17.count_s, s32[384]{0:T(512)} %owner_h.1, bf16[384,128]{1,0:T(8,128)(2,1)} %feat_h.1, bf16[128,128]{1,0:T(8,128)(2,1)} %weight_h.1, ...), custom_call_target="tpu_custom_call" | custom-call | tf_op jit(solution)/shard_map/pallas_call | solution.py:541
  64.3 0.6 copy.14
  64.9 0.6 copy.16
  65.5 0.6 copy.15

commit v5 on v4

--- a/solution.py
+++ b/solution.py
@@ -36,7 +36,7 @@
     og_m, og_c, og_g, og_z,
     ac_m, ac_z, ac_g, ac_c,
     sx_out, sy_out, sx_in, sy_in, x_out, y_out, x_in, y_in, x2_out, y2_out, x2_in, y2_in,
-    dgrad, gath, hg_out, hg_in, dw, dw_in, dw_all, dw_full, spare,
+    dgrad, gath, hg_out, hg_in, dw, dw_in, dw_all, spare,
     l_sem, t_sem, i_sem,
     f_s, f_r, idz_s, idz_r, idc_s, idc_r, ogc_s, ogc_r, ogz_s, ogz_r, acz_s, acz_r, acc_s, acc_r,
     sx_s, sx_r, sy_s, sy_r, rx_s, rx_r, ry_s, ry_r, rx2_s, rx2_r, ry2_s, ry2_r,
@@ -445,8 +445,11 @@
     act_out[...] = mm(pick_t[...], came).astype(BF16)
     ones = jnp.where((iota((16, 512), 1) & 3) == 3, 1.0, 0.0).astype(BF16)
     mine = mm(ones, came)[0:1] * (1.0 / math.sqrt(49152.0))
-    dw_all[x, y, e] = mine
-    w_copies = [send(dw_all.at[x, y, e], dw_all.at[x, y, e], wg_s.at[0], wg_r.at[0], sibling)]
+    dw_all[r, x, y, e] = mine
+    w_copies = []
+    for d in (2, 1, 3):
+        part = dw_all.at[r, x, y, e]
+        w_copies.append(send(part, part, wa_s.at[d - 1], wa_r.at[d - 1], {"row": lax.rem(r + d, 4), "col": c}))
     for cp in asib:
         cp.wait_recv()
 
@@ -459,21 +462,20 @@
         return carry
     lax.fori_loop(0, 128 // UNROLL, backward, 0)
 
-    w_copies[0].wait_recv()
-    for d in (2, 1, 3):
-        part = dw_all.at[x, y]
-        w_copies.append(send(part, part, wg_s.at[d], wg_r.at[d], at_chip(lax.rem(x + d, 4), y)))
+    for cp in w_copies:
+        cp.wait_recv()
+    part = dw_all.at[:, x, y, e]
+    w_copies.append(send(part, part, wg_s.at[0], wg_r.at[0], sibling))
     lax.fori_loop(128 // UNROLL, 256 // UNROLL, backward, 0)
 
     def finish(pos):
         for j in range(3):
             hg_out[pos, pl.ds(j * 128, 128), :] = run[lasts_s[0, pos * 3 + j]].astype(BF16)
 
-    for cp in w_copies[1:]:
-        cp.wait_recv()
-    for d in (2, 1, 3):
-        part = dw_all.at[:, y]
-        w_copies.append(send(part, part, wg_s.at[3 + d], wg_r.at[3 + d], at_chip(x, lax.rem(y + d, 4))))
+    w_copies[3].wait_recv()
+    for d in (2, 1, 3):
+        part = dw_all.at[:, x, y]
+        w_copies.append(send(part, part, wg_s.at[d], wg_r.at[d], at_chip(lax.rem(x + d, 4), y)))
 
     hgc = []
     for d in (2, 1, 3):
@@ -484,8 +486,9 @@
 
     for cp in w_copies[4:]:
         cp.wait_recv()
-    dw_full[r] = dw_all[...].reshape(32, 128)
-    wa = to_rows(lambda to: dw_full.at[r], dw_full, wa_s, wa_r)
+    for d in (2, 1, 3):
+        part = dw_all.at[:, :, y]
+        w_copies.append(send(part, part, wg_s.at[3 + d], wg_r.at[3 + d], at_chip(x, lax.rem(y + d, 4))))
 
     by_y.sent()
     by_x.sent()
@@ -502,8 +505,9 @@
         fg_out[pl.ds(j * 128, 128), :] = mm(weight[...], hidden_grad[j * 128:(j + 1) * 128]).T.astype(BF16)
     for cp in hgc + w_copies:
         cp.wait_send()
-    done(wa)
-    wg_out[...] = dw_full[...].reshape(128, 128)
+    for cp in w_copies[7:]:
+        cp.wait_recv()
+    wg_out[...] = dw_all[...].reshape(128, 128)
 
 
 def local(features, weight, tiles, tile_dest, tile_src, tile_count, source_of, out_grad):
@@ -528,7 +532,7 @@
         V(4, 4, 192, 128), V(4, 4, 192, 128), V(6, 2, 192, 128), V(6, 2, 192, 128),
         V(4, 192, 128), V(4, 192, 128), V(4, 192, 128), V(4, 192, 128),
         V(384, 128, dtype=F32), V(4, 4, 2, 2, 192, 128), V(4, 384, 128), V(3, 384, 128),
-        V(4, 32, 128, dtype=F32), V(4, 32, 128, dtype=F32), V(4, 4, 2, 1, 128, dtype=F32), V(4, 32, 128, dtype=F32), V(512, 96),
+        V(4, 32, 128, dtype=F32), V(4, 32, 128, dtype=F32), V(4, 4, 4, 2, 1, 128, dtype=F32), V(512, 96),
         D(8), D(4), D(4),
         D(6), D(6), D(3), D(3), D(), D(), D(), D(), D(3), D(3), D(3), D(3), D(), D(),
         D(4), D(4), D(4), D(4), D(6), D(6), D(6), D(6), D(3), D(3), D(3), D(3),

time: 66.3 us -> 65.6 us (0.989)
  Pallas kernels: 63 us -> 61.9 us
    pallas_call x1, Pallas kernels: 63 us -> 61.9 us  [local(): pl.pallas_call(kernel, out_shape=(pltpu.VMEM((384, 128), BF16), pltpu.VME...]
where the time goes in v5:
time: 65.6 us; the launch traced here: 65.1 us
  Pallas kernels  61.9 us (94%)
  local copies, waits for them, and re-layouts  1.91 us (3%)
  between operations  1.29 us (2%)
    pallas_call x1, Pallas kernels, local(): pl.pallas_call(kernel, out_shape=(pltpu.VMEM((384, 128), BF16), pltpu.VME...  61.9 us
    unnamed x3, local copies, waits for them, and re-layouts  1.91 us

profile of v5, /device:TPU:1, one launch (start us, length us, event | category | flops | bytes accessed | tf_op | source)
XLA Modules:
  0.0 65.1 jit_solution(5176428738387427863)
XLA Ops:
  1.3 61.9 %shard_map.103 = (bf16[384,128]{1,0:T(8,128)(2,1)S(1)}, bf16[384,128]{1,0:T(8,128)(2,1)S(1)}, f32[128,128]{1,0:T(8,128)S(1)}) custom-call(s32[1,256]{1,0:T(1,128)} %dest_h.1, s32[1,256]{1,0:T(1,128)} %src_h.1, s32[1,1]{1,0:T(1,128)S(6)} %copy.17.count_s, s32[384]{0:T(512)} %owner_h.1, bf16[384,128]{1,0:T(8,128)(2,1)} %feat_h.1, bf16[128,128]{1,0:T(8,128)(2,1)} %weight_h.1, ...), custom_call_target="tpu_custom_call" | custom-call | tf_op jit(solution)/shard_map/pallas_call | solution.py:545
  63.2 0.6 copy.14
  63.8 0.6 copy.16
  64.4 0.6 copy.15
